TPU v7x, 256 devices: a whole 4x4x8 slice. The times are simulated.
256 devices in a mesh: sx: 32 (over y_lo, z, core), sy: 4 (over x), ch: 2 (over y_hi).
Axes of the slice: x: 4, y: 4 (y_hi: 2, y_lo: 2; y = y_hi * 2 + y_lo), z: 8, core: 2. Of those that a mesh axis runs over, the one named last changes fastest.
Arguments:
- volume: bfloat16 [4, 256, 16, 512], P(None, ('sx', 'ch'), 'sy'), may hold values from -6 to 6
- w_first: bfloat16 [32, 108], replicated, may hold values from -0.625 to 0.625
- w_second: bfloat16 [64, 864], replicated, may hold values from -0.21875 to 0.21875
- w_third: bfloat16 [128, 1728], replicated, may hold values from -0.15625 to 0.15625
- w_deep: bfloat16 [256, 3456], P(('sy', 'ch')), may hold values from -0.109375 to 0.109375
- grad_out: bfloat16 [256, 64, 4, 128], P(('sy', 'ch'), 'sx'), may hold values from -6 to 6
Outputs:
- activ: bfloat16 [256, 64, 4, 128], P(('sy', 'ch'), 'sx')
- grad_w1: float32 [32, 108], replicated
- grad_w2: float32 [64, 864], replicated
- grad_w3: float32 [128, 1728], replicated
- grad_w4: float32 [256, 3456], P(('sy', 'ch'))
All inputs are finite; a program needn't handle non-finite values.
Results may differ from a plain program's by a relative error of at most 0.03.
Values may be sent and summed in bfloat16 or wider, within the bound.
A program may use at most 128 MiB of HBM per device.

v0:
```python
import jax
import jax.numpy as jnp
from jax import lax
from jax.sharding import PartitionSpec as P


def shifted(value, axis, by):
    length = lax.axis_size(axis)
    pairs = [(i, i + by) for i in range(length) if 0 <= i + by < length]
    return lax.ppermute(value, axis, pairs)


def padded_2(value, sides, width):
    for axis, dim in sides:
        size, length = (lax.axis_size(axis), value.shape[dim])
        up = [(i, (i + 1) % size) for i in range(size - 1)]
        down = [(j, i) for i, j in up]
        last = lax.slice_in_dim(value, length - width, length, axis=dim)
        first = lax.slice_in_dim(value, 0, width, axis=dim)
        before = lax.ppermute(last, axis, up)
        after = lax.ppermute(first, axis, down)
        value = jnp.concatenate([before, value, after], axis=dim)
    return value


def smooth_unit(values):
    return 0.3 * values + 0.7 * values * jax.nn.sigmoid(values)


def smooth_slope(values):
    sigma = jax.nn.sigmoid(values)
    return 0.3 + 0.7 * (sigma + values * sigma * (1.0 - sigma))


def tap_block(padded, depth_tap, extent, stride):
    depth, height, width = extent
    pieces = []
    for row_tap in range(3):
        for col_tap in range(3):
            pieces.append(
                padded[
                    :,
                    depth_tap : depth_tap + stride * (depth - 1) + 1 : stride,
                    row_tap : row_tap + stride * (height - 1) + 1 : stride,
                    col_tap : col_tap + stride * (width - 1) + 1 : stride,
                ]
            )
    stacked = jnp.concatenate(pieces, axis=0)
    return stacked.reshape(stacked.shape[0], depth * height * width)


def conv_apply(padded, weight, extent, stride):
    channels = padded.shape[0]
    summed = None
    for depth_tap in range(3):
        stacked = tap_block(padded, depth_tap, extent, stride)
        columns = weight[:, depth_tap * 9 * channels : (depth_tap + 1) * 9 * channels]
        partial_sum = jnp.dot(columns, stacked, preferred_element_type=jnp.float32)
        summed = partial_sum if summed is None else summed + partial_sum
    return summed.reshape((weight.shape[0],) + tuple(extent))


def weight_grad(padded, cotangent, extent, stride):
    flattened = cotangent.reshape(cotangent.shape[0], -1)
    pieces = []
    for depth_tap in range(3):
        stacked = tap_block(padded, depth_tap, extent, stride)
        pieces.append(
            lax.dot_general(
                flattened, stacked, (((1,), (1,)), ((), ())), preferred_element_type=jnp.float32
            )
        )
    return jnp.concatenate(pieces, axis=1)


def flipped(weight):
    filters = weight.shape[0]
    channels = weight.shape[1] // 27
    shaped = weight.reshape(filters, 27, channels)[:, ::-1, :]
    return jnp.transpose(shaped, (2, 1, 0)).reshape(channels, 27 * filters)


def lower_rims(field):
    plane = shifted(field[:, -1:], ("sx", "ch"), 1)
    field = jnp.concatenate([plane, field], axis=1)
    row_rim = shifted(field[:, :, -1:], "sy", 1)
    field = jnp.concatenate([row_rim, field], axis=2)
    return jnp.pad(field, ((0, 0), (0, 0), (0, 0), (1, 0)))


def upper_rims(field):
    plane = shifted(field, ("sx", "ch"), -1)
    field = jnp.concatenate([field, plane], axis=1)
    row_rim = shifted(field, "sy", -1)
    field = jnp.concatenate([field, row_rim], axis=2)
    return jnp.pad(field, ((0, 0), (0, 0), (0, 0), (0, 1)))


def margins(field):
    padded = padded_2(field, ((("sx", "ch"), 1), ("sy", 2)), 1)
    return jnp.pad(padded, ((0, 0), (0, 0), (0, 0), (1, 1)))


def deep_margins(field):
    padded = padded_2(field, (("sx", 1),), 1)
    return jnp.pad(padded, ((0, 0), (0, 0), (1, 1), (1, 1)))


def spread_back(padded, weight, extent):
    depth, height, width = extent
    filters = padded.shape[0]
    channels = weight.shape[1] // 27
    kernel = weight.reshape(weight.shape[0], 27, channels)
    parity_taps = (((1, 0),), ((0, 1), (2, 0)))
    classes = []
    for depth_par in range(2):
        for row_par in range(2):
            for col_par in range(2):
                column_list = []
                weight_list = []
                for depth_tap, depth_off in parity_taps[depth_par]:
                    for row_tap, row_off in parity_taps[row_par]:
                        for col_tap, col_off in parity_taps[col_par]:
                            piece = padded[
                                :,
                                depth_off : depth_off + depth,
                                row_off : row_off + height,
                                col_off : col_off + width,
                            ]
                            column_list.append(piece.reshape(filters, depth * height * width))
                            weight_list.append(kernel[:, 9 * depth_tap + 3 * row_tap + col_tap, :])
                stacked = jnp.concatenate(column_list, axis=0)
                weight_stack = jnp.concatenate(weight_list, axis=0)
                classes.append(
                    lax.dot_general(
                        weight_stack,
                        stacked,
                        (((0,), (0,)), ((), ())),
                        preferred_element_type=jnp.float32,
                    )
                )
    merged = jnp.stack(classes, axis=0).reshape(2, 2, 2, channels, depth, height, width)
    merged = jnp.transpose(merged, (3, 4, 0, 5, 1, 6, 2))
    return merged.reshape(channels, 2 * depth, 2 * height, 2 * width)


def to_deep(pieces, groups_sy, groups_ch):
    count, channels, depth, height, width = pieces.shape
    shaped = pieces.reshape(groups_sy, groups_ch, channels, depth, height, width)
    shaped = jnp.transpose(shaped, (2, 1, 3, 0, 4, 5))
    return shaped.reshape(channels, groups_ch * depth, groups_sy * height, width)


def from_deep(field, groups_sy, groups_ch):
    channels, depth_all, height_all, width = field.shape
    depth = depth_all // groups_ch
    height = height_all // groups_sy
    shaped = field.reshape(channels, groups_ch, depth, groups_sy, height, width)
    shaped = jnp.transpose(shaped, (3, 1, 0, 2, 4, 5))
    return shaped.reshape(groups_sy * groups_ch, channels, depth, height, width)


def per_device(volume, w_first, w_second, w_third, w_deep, grad_out):
    groups_sy = lax.axis_size("sy")
    groups_ch = lax.axis_size("ch")
    depth_in, height_in, width_in = (volume.shape[1], volume.shape[2], volume.shape[3])
    extent_one = (depth_in // 2, height_in // 2, width_in // 2)
    extent_two = (depth_in // 4, height_in // 4, width_in // 4)
    padded_vol = lower_rims(volume)
    pre_one = conv_apply(padded_vol, w_first, extent_one, 2)
    act_one = smooth_unit(pre_one).astype(jnp.bfloat16)
    padded_one = lower_rims(act_one)
    pre_two = conv_apply(padded_one, w_second, extent_two, 2)
    act_two = smooth_unit(pre_two).astype(jnp.bfloat16)
    padded_two = margins(act_two)
    pre_three = conv_apply(padded_two, w_third, extent_two, 1)
    act_three = smooth_unit(pre_three).astype(jnp.bfloat16)
    gathered = lax.all_gather(act_three[None], ("sy", "ch"), axis=0, tiled=True)
    deep_input = to_deep(gathered, groups_sy, groups_ch)
    extent_deep = deep_input.shape[1:]
    padded_deep = deep_margins(deep_input)
    pre_deep = conv_apply(padded_deep, w_deep, extent_deep, 1)
    activ = smooth_unit(pre_deep).astype(jnp.bfloat16)
    cells_all = extent_deep[0] * lax.axis_size("sx") * extent_deep[1] * extent_deep[2]
    scale = 1.0 / float(cells_all) ** 0.5
    grad_deep = (grad_out.astype(jnp.float32) * smooth_slope(pre_deep) * scale).astype(jnp.bfloat16)
    local_w4 = weight_grad(padded_deep, grad_deep, extent_deep, 1)
    padded_grad = padded_2(grad_deep, (("sx", 1),), 1)
    padded_grad = jnp.pad(padded_grad, ((0, 0), (0, 0), (1, 1), (1, 1)))
    partial_back = conv_apply(padded_grad, flipped(w_deep), extent_deep, 1)
    pieces = from_deep(partial_back, groups_sy, groups_ch)
    back_three = lax.psum_scatter(
        pieces.astype(jnp.bfloat16), ("sy", "ch"), scatter_dimension=0, tiled=True
    ).astype(jnp.float32)[0]
    grad_three = (back_three * smooth_slope(pre_three)).astype(jnp.bfloat16)
    local_w3 = weight_grad(padded_two, grad_three, extent_two, 1)
    padded_three = margins(grad_three)
    back_two = conv_apply(padded_three, flipped(w_third), extent_two, 1)
    grad_two = (back_two * smooth_slope(pre_two)).astype(jnp.bfloat16)
    local_w2 = weight_grad(padded_one, grad_two, extent_two, 2)
    padded_back = upper_rims(grad_two)
    back_one = spread_back(padded_back, w_second, extent_two)
    grad_one = (back_one * smooth_slope(pre_one)).astype(jnp.bfloat16)
    local_w1 = weight_grad(padded_vol, grad_one, extent_one, 2)
    grad_w1, grad_w2, grad_w3 = lax.psum((local_w1, local_w2, local_w3), ("sx", "sy", "ch"))
    grad_w4 = lax.psum(local_w4.astype(jnp.bfloat16), "sx").astype(jnp.float32)
    return (activ, grad_w1, grad_w2, grad_w3, grad_w4)


def solution(mesh):
    placed = (
        P(None, ("sx", "ch"), "sy", None),
        P(),
        P(),
        P(),
        P(("sy", "ch"), None),
        P(("sy", "ch"), "sx", None, None),
    )
    return jax.shard_map(
        per_device,
        mesh=mesh,
        in_specs=placed,
        out_specs=(P(("sy", "ch"), "sx", None, None), P(), P(), P(), P(("sy", "ch"), None)),
        check_vma=False,
    )
```

profile of v0, /device:TPU:1, one launch (start us, length us, event | category | flops | bytes accessed | tf_op | source)
XLA Modules:
  0.0 719.0 jit_solution(4661321588236960870)
XLA Ops:
  8.8 5.7 collective-permute-start
  14.5 2.0 collective-permute-done
  17.4 3.1 collective-permute-start.1
  27.2 1.0 slice.875
  29.1 1.0 slice.877
  37.8 1.0 slice.867
  46.4 1.0 slice.887
  49.6 4.0 collective-permute-start.2
  53.6 4.1 collective-permute-done.2
  57.8 4.1 collective-permute-start.3
  73.5 3.1 collective-permute-start.4
  76.6 5.4 collective-permute-start.5
  82.1 3.1 collective-permute-done.5
  85.2 4.1 collective-permute-start.6
  89.3 1.3 collective-permute-start.7
  90.6 3.5 collective-permute-done.7
  96.2 26.5 %all-gather = bf16[1024,128]{0,1:T(8,128)(2,1)S(1)} all-gather(bf16[128,128]{0,1:T(8,128)(2,1)S(1)} %get-tuple-element.150), channel_id=2, replica_groups=mesh['sx'=32,'sy'=4,'ch'=2] {'sy','ch'}, dimensions={0}, use_global_device_ids=true | all-gather | bytes 294912 | tf_op jit(solution)/shard_map/all_gather | solution.py:178
  123.2 11.1 %collective-permute-start.8 = (bf16[128,1,4,128]{3,0,2,1:T(8,128)(2,1)S(1)}, bf16[128,1,4,128]{3,0,2,1:T(8,128)(2,1)S(1)}, u32[]{:S(2)}, u32[]{:S(2)}) collective-permute-start(bf16[128,1,4,128]{3,0,2,1:T(8,128)(2,1)S(1)} %get-tuple-element.98), channel_id=1, source_target_pairs={{0,8},{8,16},{16,24},{24,32},{32,40},{40,48},{48,56},{56,64},{64,7... | collective-permute-start | bytes 393224 | tf_op jit(solution)/shard_map/ppermute | solution.py:20
  134.3 2.1 collective-permute-start.9
  137.7 3.0 collective-permute-done.9
  142.1 1.2 constant_dynamic-update-slice_fusion.152
  143.3 1.3 constant_dynamic-update-slice_fusion.151
  144.6 1.2 constant_dynamic-update-slice_fusion.150
  147.3 1.2 constant_dynamic-update-slice_fusion.148
  149.2 1.2 constant_dynamic-update-slice_fusion.147
  150.4 1.2 constant_dynamic-update-slice_fusion.146
  151.6 2.1 constant_dynamic-update-slice_fusion.145
  153.7 1.1 copy.144
  155.6 1.8 copy.145
  157.4 1.8 copy.146
  159.1 1.8 copy.147
  160.9 1.8 copy.149
  164.6 4.3 copy.143
  169.0 3.1 fusion.92
  173.0 3.0 copy.153
  176.0 1.8 constant_dynamic-update-slice_fusion.72
  177.8 1.7 constant_dynamic-update-slice_fusion.71
  179.5 1.7 constant_dynamic-update-slice_fusion.70
  182.0 1.7 constant_dynamic-update-slice_fusion.68
  186.0 2.5 convolution_add_fusion.3
  190.1 2.4 fusion.3
  192.6 2.5 fusion.5
  195.1 2.4 fusion.4
  197.6 1.9 collective-permute-start.10
  199.5 2.4 collective-permute-start.11
  202.9 2.1 collective-permute-done.11
  209.7 1.5 reshape.235
  211.3 1.5 reshape.238
  212.8 1.5 reshape.239
  217.8 200.8 %all-reduce.11.cloned.1.call-done = bf16[32,3456]{1,0:T(8,128)(2,1)} async-done(((bf16[32,3456]{1,0:T(8,128)(2,1)}), bf16[32,3456]{1,0:T(8,128)(2,1)}) %all-reduce.11.cloned.1.call-update) | async-done | bytes 221200 | tf_op jit(solution)/shard_map/psum | solution.py:206
  418.6 1.7 convert_element_type.96
  421.5 4.5 collective-permute-start.12
  426.0 2.7 collective-permute-start.13
  428.9 3.3 collective-permute-done.13
  432.2 3.1 collective-permute-start.14
  435.3 1.3 collective-permute-start.15
  437.6 3.1 collective-permute-done.15
  442.4 5.3 collective-permute-start.16
  448.6 1.3 collective-permute-start.17
  450.7 2.5 collective-permute-done.17
  456.1 78.5 %psum.28 = f32[32,108]{1,0:T(8,128)} all-reduce(f32[32,108]{1,0:T(8,128)S(1)} %pad_maximum_fusion.27), channel_id=1, replica_groups=mesh['sx'=32,'sy'=4,'ch'=2] {'sx','sy','ch'}, use_global_device_ids=true, to_apply=%region_1.2 | all-reduce | flops 3456 | bytes 27648 | tf_op jit(solution)/shard_map/psum | solution.py:205
  534.6 173.2 %all-reduce.13.cloned.1.call-done = (f32[64,864]{1,0:T(8,128)}, f32[128,1728]{0,1:T(8,128)}) async-done(((f32[64,864]{1,0:T(8,128)}, f32[128,1728]{0,1:T(8,128)}), (f32[64,864]{1,0:T(8,128)}, f32[128,1728]{0,1:T(8,128)})) %all-reduce.13.cloned.1.call-update) | async-done | bytes 1105936 | tf_op jit(solution)/shard_map/psum | solution.py:205
  707.8 1.6 copy.335
  709.4 2.1 copy.336
  (300 shorter events, 71.0 us)
Async XLA Ops:
  8.0 41.0 %copy-start.30 = (bf16[32,108]{1,0:T(8,128)(2,1)S(1)}, bf16[32,108]{1,0:T(8,128)(2,1)}, u32[]{:S(2)}) copy-start(bf16[32,108]{1,0:T(8,128)(2,1)} %param.7) | copy-start | bytes 20740
  8.0 410.6 %all-reduce.11.cloned.1.call-start = ((), (), s32[]{:S(2)}) async-start(), calls=%async_computation.2 | async-start | bytes 442368 | tf_op jit(solution)/shard_map/psum | solution.py:206
  8.8 7.6 %collective-permute-start = (bf16[4,1,4,512]{3,0,2,1:T(4,128)(2,1)S(1)}, bf16[4,1,4,512]{3,0,2,1:T(4,128)(2,1)S(1)}, u32[]{:S(2)}, u32[]{:S(2)}) collective-permute-start(bf16[4,1,4,512]{3,0,2,1:T(4,128)(2,1)S(1)} %copy.187), channel_id=1, source_target_pairs={{0,1},{1,8},{8,9},{9,16},{16,17},{17,24},{24,25},{25,32},{32,33},{... | collective-permute-start | bytes 49160 | tf_op jit(solution)/shard_map/ppermute | solution.py:10
  17.4 4.0 collective-permute-start.1
  21.5 51.4 %copy-start.17 = (bf16[64,864]{1,0:T(8,128)(2,1)S(1)}, bf16[64,864]{1,0:T(8,128)(2,1)}, u32[]{:S(2)}) copy-start(bf16[64,864]{1,0:T(8,128)(2,1)} %param.8) | copy-start | bytes 331780
  47.8 14.1 %copy-start.6 = (bf16[36,2,2,256]{3,0,2,1:T(8,128)(2,1)}, bf16[36,2,2,256]{3,0,2,1:T(8,128)(2,1)S(1)}, u32[]{:S(2)}) copy-start(bf16[36,2,2,256]{3,0,2,1:T(8,128)(2,1)S(1)} %concatenate.192) | copy-start | bytes 221188
  48.0 13.9 %copy-start.8 = (bf16[36,2,2,256]{3,0,2,1:T(8,128)(2,1)}, bf16[36,2,2,256]{3,0,2,1:T(8,128)(2,1)S(1)}, u32[]{:S(2)}) copy-start(bf16[36,2,2,256]{3,0,2,1:T(8,128)(2,1)S(1)} %concatenate.194) | copy-start | bytes 221188
  49.0 45.8 %copy-start = (bf16[128,1728]{0,1:T(8,128)(2,1)S(1)}, bf16[128,1728]{0,1:T(8,128)(2,1)}, u32[]{:S(2)}) copy-start(bf16[128,1728]{0,1:T(8,128)(2,1)} %param.9) | copy-start | bytes 1327108
  49.6 8.2 %collective-permute-start.2 = (bf16[32,1,2,256]{3,0,2,1:T(8,128)(2,1)S(1)}, bf16[32,1,2,256]{3,0,2,1:T(8,128)(2,1)S(1)}, u32[]{:S(2)}, u32[]{:S(2)}) collective-permute-start(bf16[32,1,2,256]{3,0,2,1:T(8,128)(2,1)S(1)} %slice.1072), channel_id=1, source_target_pairs={{0,1},{1,8},{8,9},{9,16},{16,17},{17,24},{24,25},{25,32},{32,33},{... | collective-permute-start | bytes 98312 | tf_op jit(solution)/shard_map/ppermute | solution.py:10
  57.8 5.1 collective-permute-start.3
  72.7 50.4 %copy-start.24 = (bf16[288,1,1,128]{3,0,2,1:T(8,128)(2,1)}, bf16[288,1,1,128]{3,0,2,1:T(8,128)(2,1)S(1)}, u32[]{:S(2)}) copy-start(bf16[288,1,1,128]{3,0,2,1:T(8,128)(2,1)S(1)} %constant_dynamic-update-slice_fusion.20) | copy-start | bytes 221188
  72.8 50.3 %copy-start.22 = (bf16[288,1,1,128]{3,0,2,1:T(8,128)(2,1)}, bf16[288,1,1,128]{3,0,2,1:T(8,128)(2,1)S(1)}, u32[]{:S(2)}) copy-start(bf16[288,1,1,128]{3,0,2,1:T(8,128)(2,1)S(1)} %constant_dynamic-update-slice_fusion.11) | copy-start | bytes 221188
  72.9 50.2 %copy-start.20 = (bf16[288,1,1,128]{3,0,2,1:T(8,128)(2,1)}, bf16[288,1,1,128]{3,0,2,1:T(8,128)(2,1)S(1)}, u32[]{:S(2)}) copy-start(bf16[288,1,1,128]{3,0,2,1:T(8,128)(2,1)S(1)} %constant_dynamic-update-slice_fusion.2) | copy-start | bytes 221188
  73.5 49.7 %copy-start.26 = (f32[64,128]{1,0:T(8,128)}, f32[64,128]{1,0:T(8,128)S(1)}, u32[]{:S(2)}) copy-start(f32[64,128]{1,0:T(8,128)S(1)} %fusion.13) | copy-start | bytes 98308
  73.5 8.5 %collective-permute-start.4 = (bf16[64,1,1,128]{3,0,2,1:T(8,128)(2,1)S(1)}, bf16[64,1,1,128]{3,0,2,1:T(8,128)(2,1)S(1)}, u32[]{:S(2)}, u32[]{:S(2)}) collective-permute-start(bf16[64,1,1,128]{3,0,2,1:T(8,128)(2,1)S(1)} %fusion.132), channel_id=1, source_target_pairs={{0,1},{1,8},{8,9},{9,16},{16,17},{17,24},{24,25},{25,32},{32,33},{... | collective-permute-start | bytes 49160 | tf_op jit(solution)/shard_map/ppermute | solution.py:20
  76.6 8.6 %collective-permute-start.5 = (bf16[64,1,1,128]{3,0,2,1:T(8,128)(2,1)S(1)}, bf16[64,1,1,128]{3,0,2,1:T(8,128)(2,1)S(1)}, u32[]{:S(2)}, u32[]{:S(2)}) collective-permute-start(bf16[64,1,1,128]{3,0,2,1:T(8,128)(2,1)S(1)} %fusion.132), channel_id=1, source_target_pairs={{1,0},{8,1},{9,8},{16,9},{17,16},{24,17},{25,24},{32,25},{33,32},{... | collective-permute-start | bytes 49160 | tf_op jit(solution)/shard_map/ppermute | solution.py:21
  85.2 51.3 %copy-start.4 = (bf16[32,3456]{1,0:T(8,128)(2,1)S(1)}, bf16[32,3456]{1,0:T(8,128)(2,1)}, u32[]{:S(2)}) copy-start(bf16[32,3456]{1,0:T(8,128)(2,1)} %param.10) | copy-start | bytes 663556
  85.2 5.4 collective-permute-start.6
  89.3 4.8 collective-permute-start.7
  94.8 28.4 %copy-start.28 = (bf16[576,1,1,128]{3,0,2,1:T(8,128)(2,1)}, bf16[576,1,1,128]{3,0,2,1:T(8,128)(2,1)S(1)}, u32[]{:S(2)}) copy-start(bf16[576,1,1,128]{3,0,2,1:T(8,128)(2,1)S(1)} %get-tuple-element.80) | copy-start | bytes 442372
  94.8 39.5 %copy-start.13 = (bf16[576,1,1,128]{3,0,2,1:T(8,128)(2,1)}, bf16[576,1,1,128]{3,0,2,1:T(8,128)(2,1)S(1)}, u32[]{:S(2)}) copy-start(bf16[576,1,1,128]{3,0,2,1:T(8,128)(2,1)S(1)} %get-tuple-element.81) | copy-start | bytes 442372
  94.8 39.5 %copy-start.15 = (bf16[576,1,1,128]{3,0,2,1:T(8,128)(2,1)}, bf16[576,1,1,128]{3,0,2,1:T(8,128)(2,1)S(1)}, u32[]{:S(2)}) copy-start(bf16[576,1,1,128]{3,0,2,1:T(8,128)(2,1)S(1)} %get-tuple-element.82) | copy-start | bytes 442372
  123.2 14.5 %collective-permute-start.8 = (bf16[128,1,4,128]{3,0,2,1:T(8,128)(2,1)S(1)}, bf16[128,1,4,128]{3,0,2,1:T(8,128)(2,1)S(1)}, u32[]{:S(2)}, u32[]{:S(2)}) collective-permute-start(bf16[128,1,4,128]{3,0,2,1:T(8,128)(2,1)S(1)} %get-tuple-element.98), channel_id=1, source_target_pairs={{0,8},{8,16},{16,24},{24,32},{32,40},{40,48},{48,56},{56,64},{64,7... | collective-permute-start | bytes 393224 | tf_op jit(solution)/shard_map/ppermute | solution.py:20
  134.3 6.3 collective-permute-start.9
  176.0 7.7 %copy-start.2 = (bf16[128,2,4,128]{0,3,2,1:T(8,128)(2,1)S(1)}, bf16[128,2,4,128]{0,3,2,1:T(8,128)(2,1)}, u32[]{:S(2)}) copy-start(bf16[128,2,4,128]{0,3,2,1:T(8,128)(2,1)} %copy.150) | copy-start | bytes 786436
  176.0 8.5 %copy-start.1 = (bf16[128,2,4,128]{0,3,2,1:T(8,128)(2,1)S(1)}, bf16[128,2,4,128]{0,3,2,1:T(8,128)(2,1)}, u32[]{:S(2)}) copy-start(bf16[128,2,4,128]{0,3,2,1:T(8,128)(2,1)} %copy.151) | copy-start | bytes 786436
  176.0 9.9 %copy-start.5 = (bf16[32,3456]{1,0:T(8,128)(2,1)S(1)}, bf16[32,3456]{1,0:T(8,128)(2,1)}, u32[]{:S(2)}) copy-start(bf16[32,3456]{1,0:T(8,128)(2,1)} %param.10) | copy-start | bytes 663556
  176.0 9.9 %copy-start.19 = (f32[1024,32]{0,1:T(8,128)S(1)}, f32[1024,32]{0,1:T(8,128)}, u32[]{:S(2)}) copy-start(f32[1024,32]{0,1:T(8,128)} %fusion.92) | copy-start | bytes 393220
  186.0 3.4 copy-start.31
  197.6 5.4 collective-permute-start.10
  199.5 5.5 collective-permute-start.11
  202.6 217.7 %reduce-scatter.2.cloned.1.call-start = ((), (), s32[]{:S(2)}) async-start(), calls=%async_computation.1 | async-start | bytes 294912 | tf_op jit(solution)/shard_map/reduce_scatter | solution.py:192
  206.5 7.8 %copy-start.3 = (bf16[128,27,32]{0,2,1:T(8,128)(2,1)S(1)}, bf16[128,27,32]{0,2,1:T(8,128)(2,1)}, u32[]{:S(2)}) copy-start(bf16[128,27,32]{0,2,1:T(8,128)(2,1)} %copy.154) | copy-start | bytes 663556
  207.3 0.8 copy-start.10
  208.1 0.8 copy-start.11
  208.9 0.8 copy-start.12
  214.3 2.1 copy-start.18
  216.3 204.0 %copy-start.32 = (f32[128,128]{0,1:T(8,128)S(1)}, f32[128,128]{0,1:T(8,128)}, u32[]{:S(2)}) copy-start(f32[128,128]{0,1:T(8,128)} %get-tuple-element.151) | copy-start | bytes 196612
  216.4 204.8 %copy-start.29 = (bf16[576,1,1,128]{3,0,2,1:T(8,128)(2,1)S(1)}, bf16[576,1,1,128]{3,0,2,1:T(8,128)(2,1)}, u32[]{:S(2)}) copy-start(bf16[576,1,1,128]{3,0,2,1:T(8,128)(2,1)} %copy-done.28) | copy-start | bytes 442372
  216.4 491.4 %all-reduce.13.cloned.1.call-start = ((), (), s32[]{:S(2)}) async-start(), calls=%async_computation.3 | async-start | bytes 2228224 | tf_op jit(solution)/shard_map/psum | solution.py:205
  216.6 204.8 %copy-start.14 = (bf16[576,1,1,128]{3,0,2,1:T(8,128)(2,1)S(1)}, bf16[576,1,1,128]{3,0,2,1:T(8,128)(2,1)}, u32[]{:S(2)}) copy-start(bf16[576,1,1,128]{3,0,2,1:T(8,128)(2,1)} %copy-done.13) | copy-start | bytes 442372
  216.9 211.8 %copy-start.16 = (bf16[576,1,1,128]{3,0,2,1:T(8,128)(2,1)S(1)}, bf16[576,1,1,128]{3,0,2,1:T(8,128)(2,1)}, u32[]{:S(2)}) copy-start(bf16[576,1,1,128]{3,0,2,1:T(8,128)(2,1)} %copy-done.15) | copy-start | bytes 442372
  421.5 7.4 %collective-permute-start.12 = (bf16[128,1,1,128]{0,3,2,1:T(8,128)(2,1)S(1)}, bf16[128,1,1,128]{0,3,2,1:T(8,128)(2,1)S(1)}, u32[]{:S(2)}, u32[]{:S(2)}) collective-permute-start(bf16[128,1,1,128]{0,3,2,1:T(8,128)(2,1)S(1)} %bitcast.286), channel_id=1, source_target_pairs={{0,1},{1,8},{8,9},{9,16},{16,17},{17,24},{24,25},{25,32},{32,33},{... | collective-permute-start | bytes 98312 | tf_op jit(solution)/shard_map/ppermute | solution.py:20
  426.0 6.2 collective-permute-start.13
  432.2 9.4 %copy-start.27 = (f32[64,128]{1,0:T(8,128)S(1)}, f32[64,128]{1,0:T(8,128)}, u32[]{:S(2)}) copy-start(f32[64,128]{1,0:T(8,128)} %copy-done.26) | copy-start | bytes 98308
  432.2 5.4 collective-permute-start.14
  435.3 5.4 collective-permute-start.15
  437.6 4.3 copy-start.23
  437.6 4.5 copy-start.25
  437.6 4.6 copy-start.21
  442.4 6.2 collective-permute-start.16
  448.6 4.6 collective-permute-start.17
  450.7 4.9 copy-start.7
  450.7 5.2 copy-start.9
Sparse Core Ops, SparseCore 0:
  202.7 215.8 all-reduce.10
Sparse Core Ops, SparseCore 1:
  216.4 75.3 reduce-scatter.1
  450.8 256.9 all-reduce.12
where the time goes:
time: 721 us; the launch traced here: 719 us
  waiting for transfers between devices  403 us (56%)
  blocking collectives  105 us (15%)
  local copies, waits for them, and re-layouts  95.9 us (13%)
  starting transfers between devices  66.9 us (9%)
  matrix products  21.7 us (3%)
  between operations  16.9 us (2%)
  other arithmetic  9.2 us (1%)
    psum x1, waiting for transfers between devices, per_device(): grad_w4 = lax.psum(local_w4.astype(jnp.bfloat16), 'sx').astype(jnp.float32)  201 us
    psum x1, waiting for transfers between devices, per_device(): lax.psum((local_w1, local_w2, local_w3), ('sx', 'sy', 'ch'))  173 us
    psum x1, blocking collectives, per_device(): lax.psum((local_w1, local_w2, local_w3), ('sx', 'sy', 'ch'))  78.5 us
    slice x62, local copies, waits for them, and re-layouts, tap_block(): padded[:, depth_tap:depth_tap + stride * (depth - 1) + 1:stride, row_tap:...  45.4 us
    unnamed x144, local copies, waits for them, and re-layouts  28.1 us
    ppermute x6, starting transfers between devices, padded_2(): before = lax.ppermute(last, axis, up)  27.8 us
    all_gather x1, blocking collectives, per_device(): gathered = lax.all_gather(act_three[None], ('sy', 'ch'), axis=0, tiled=True)  26.5 us
    ppermute x6, starting transfers between devices, shifted(): return lax.ppermute(value, axis, pairs)  23.5 us
  transfers between devices with their start and end apart: 21, of which 14 were waited for; matrix products, arithmetic and copies ran while one was open for 3% of the time, Pallas kernels for 0%

commit v1 on v0

--- a/solution.py
+++ b/solution.py
@@ -1,7 +1,210 @@
+import functools
 import jax
 import jax.numpy as jnp
 from jax import lax
+from jax.experimental import pallas as pl
+from jax.experimental.pallas import tpu as pltpu
 from jax.sharding import PartitionSpec as P
+
+MESH = pl.DeviceIdType.MESH
+BF = jnp.bfloat16
+F32 = jnp.float32
+N3, N2, N4 = 27, 30, 27
+
+
+def plane_place(rank, z):
+    sy = lax.rem(rank, 4)
+    ch = lax.rem(lax.div(rank, 4), 2)
+    core = lax.rem(lax.div(rank, 8), 2)
+    low = lax.div(rank, 16)
+    return (low * 16 + z * 2 + core, sy, ch)
+
+
+def await_bytes(ref, sem):
+    pltpu.make_async_copy(ref, ref, sem).wait()
+
+
+def sum_kernel(
+    a3, a2, a4, o3, o2, o4,
+    in3, in2, in4, mid3, mid2, part3, part2, all3, all2, all4,
+    send, recv,
+):
+    sx, sy, ch = lax.axis_index("sx"), lax.axis_index("sy"), lax.axis_index("ch")
+    core = lax.rem(sx, 2)
+    z = lax.rem(lax.div(sx, 2), 8)
+    low = lax.div(sx, 16)
+    rank = low * 16 + core * 8 + ch * 4 + sy
+
+    def plane(k):
+        other = lax.rem(rank + k, 32)
+        return other, plane_place(other, z)
+
+    def column(k):
+        other = lax.rem(z + k, 8)
+        return other, (low * 16 + other * 2 + core, sy, ch)
+
+    def depth(k):
+        other = lax.rem(sx + k, 32)
+        return other, (other, sy, ch)
+
+    barrier = pltpu.get_barrier_semaphore()
+
+    def greet(count, where):
+        def step(k, carry):
+            pl.semaphore_signal(barrier, inc=1, device_id=where(k)[1], device_id_type=MESH)
+            return carry
+        lax.fori_loop(1, count, step, 0)
+
+    greet(32, plane)
+    greet(8, column)
+    greet(32, depth)
+    pl.semaphore_wait(barrier, 31 + 7 + 31)
+
+    def scatter(count, where, shards, src, dst, mine, slot):
+        def step(k, carry):
+            other, place = where(k)
+
+            @pl.when(other < shards)
+            def _():
+                pltpu.make_async_remote_copy(
+                    src_ref=src.at[other], dst_ref=dst.at[mine],
+                    send_sem=send.at[slot], recv_sem=recv.at[slot],
+                    device_id=place, device_id_type=MESH,
+                ).start()
+            return carry
+        lax.fori_loop(1, count, step, 0)
+
+    def spread(count, where, src, dst, slot):
+        def step(k, carry):
+            other, place = where(k)
+            pltpu.make_async_remote_copy(
+                src_ref=src, dst_ref=dst,
+                send_sem=send.at[slot], recv_sem=recv.at[slot],
+                device_id=place, device_id_type=MESH,
+            ).start()
+            return carry
+        lax.fori_loop(1, count, step, 0)
+
+    def total(ref, count):
+        def step(i, acc):
+            return acc + ref[i].astype(F32)
+        return lax.fori_loop(0, count, step, jnp.zeros(ref.shape[1:], F32))
+
+    scatter(32, plane, N2, a2, in2, rank, 0)
+    scatter(32, plane, N3, a3, in3, rank, 1)
+    scatter(32, depth, N4, a4, in4, sx, 2)
+
+    @pl.when(rank < N2)
+    def _():
+        in2[rank] = a2[rank]
+        await_bytes(in2.at[pl.ds(0, 31)], recv.at[0])
+        part2[...] = total(in2, 32).astype(BF)
+        mid2[z] = part2[...]
+        spread(8, column, part2, mid2.at[z], 3)
+
+    @pl.when(rank < N3)
+    def _():
+        in3[rank] = a3[rank]
+        await_bytes(in3.at[pl.ds(0, 31)], recv.at[1])
+        part3[...] = total(in3, 32).astype(BF)
+        mid3[z] = part3[...]
+        spread(8, column, part3, mid3.at[z], 4)
+
+    @pl.when(sx < N4)
+    def _():
+        in4[sx] = a4[sx]
+        await_bytes(in4.at[pl.ds(0, 31)], recv.at[2])
+        all4[sx] = total(in4, 32).astype(BF)
+        spread(32, depth, all4.at[sx], all4.at[sx], 5)
+
+    @pl.when(rank < N2)
+    def _():
+        await_bytes(mid2.at[pl.ds(0, 7)], recv.at[3])
+        all2[rank] = total(mid2, 8).astype(BF)
+        spread(32, plane, all2.at[rank], all2.at[rank], 6)
+
+    @pl.when(rank < N3)
+    def _():
+        await_bytes(mid3.at[pl.ds(0, 7)], recv.at[4])
+        all3[rank] = total(mid3, 8).astype(BF)
+        spread(32, plane, all3.at[rank], all3.at[rank], 7)
+
+    def finish(me, shards, buf, out, slot):
+        @pl.when(me < shards)
+        def _():
+            await_bytes(buf.at[pl.ds(0, shards - 1)], recv.at[slot])
+
+        @pl.when(me >= shards)
+        def _():
+            await_bytes(buf.at[pl.ds(0, shards)], recv.at[slot])
+
+        def step(i, carry):
+            out[i] = buf[i].astype(F32)
+            return carry
+        lax.fori_loop(0, shards, step, 0)
+
+    finish(sx, N4, all4, o4, 5)
+    finish(rank, N2, all2, o2, 6)
+    finish(rank, N3, all3, o3, 7)
+
+    def sent(me, shards, src, slot):
+        @pl.when(me < shards)
+        def _():
+            await_bytes(src.at[pl.ds(0, shards - 1)], send.at[slot])
+
+        @pl.when(me >= shards)
+        def _():
+            await_bytes(src.at[pl.ds(0, shards)], send.at[slot])
+
+    sent(rank, N2, a2, 0)
+    sent(rank, N3, a3, 1)
+    sent(sx, N4, a4, 2)
+
+    @pl.when(rank < N2)
+    def _():
+        await_bytes(mid2.at[pl.ds(0, 7)], send.at[3])
+        await_bytes(in2.at[pl.ds(0, 31)], send.at[6])
+
+    @pl.when(rank < N3)
+    def _():
+        await_bytes(mid3.at[pl.ds(0, 7)], send.at[4])
+        await_bytes(in3.at[pl.ds(0, 31)], send.at[7])
+
+    @pl.when(sx < N4)
+    def _():
+        await_bytes(in4.at[pl.ds(0, 31)], send.at[5])
+
+
+def sum_all(a3, a2, a4):
+    vmem = pl.BlockSpec(memory_space=pltpu.VMEM)
+    return pl.pallas_call(
+        sum_kernel,
+        out_shape=(
+            jax.ShapeDtypeStruct((N3, 64, 128), F32),
+            jax.ShapeDtypeStruct((N2, 16, 128), F32),
+            jax.ShapeDtypeStruct((N4, 32, 128), F32),
+        ),
+        in_specs=[vmem] * 3,
+        out_specs=(vmem,) * 3,
+        scratch_shapes=[
+            pltpu.VMEM((32, 64, 128), BF),
+            pltpu.VMEM((32, 16, 128), BF),
+            pltpu.VMEM((32, 32, 128), BF),
+            pltpu.VMEM((8, 64, 128), BF),
+            pltpu.VMEM((8, 16, 128), BF),
+            pltpu.VMEM((64, 128), BF),
+            pltpu.VMEM((16, 128), BF),
+            pltpu.VMEM((N3, 64, 128), BF),
+            pltpu.VMEM((N2, 16, 128), BF),
+            pltpu.VMEM((N4, 32, 128), BF),
+            pltpu.SemaphoreType.DMA((8,)),
+            pltpu.SemaphoreType.DMA((8,)),
+        ],
+        compiler_params=pltpu.CompilerParams(
+            collective_id=1, has_side_effects=True, vmem_limit_bytes=32 * 1024 * 1024
+        ),
+        name="sum_filter_gradients",
+    )(a3, a2, a4)
 
 
 def shifted(value, axis, by):
@@ -202,8 +405,16 @@
     back_one = spread_back(padded_back, w_second, extent_two)
     grad_one = (back_one * smooth_slope(pre_one)).astype(jnp.bfloat16)
     local_w1 = weight_grad(padded_vol, grad_one, extent_one, 2)
-    grad_w1, grad_w2, grad_w3 = lax.psum((local_w1, local_w2, local_w3), ("sx", "sy", "ch"))
-    grad_w4 = lax.psum(local_w4.astype(jnp.bfloat16), "sx").astype(jnp.float32)
+    a3 = jnp.transpose(local_w3.astype(BF).reshape(128, 27, 64), (1, 2, 0))
+    wide2 = jnp.pad(local_w2.astype(BF), ((0, 0), (0, 32))).reshape(4, 16, 7, 128)
+    wide1 = jnp.pad(local_w1.astype(BF), ((0, 0), (0, 20))).reshape(2, 16, 128)
+    a2 = jnp.concatenate([jnp.transpose(wide2, (2, 0, 1, 3)).reshape(28, 16, 128), wide1], axis=0)
+    a4 = jnp.transpose(local_w4.astype(BF).reshape(32, 27, 128), (1, 0, 2))
+    s3, s2, s4 = sum_all(a3, a2, a4)
+    grad_w3 = jnp.transpose(s3, (2, 0, 1)).reshape(128, 1728)
+    grad_w2 = jnp.transpose(s2[:28].reshape(7, 4, 16, 128), (1, 2, 0, 3)).reshape(64, 896)[:, :864]
+    grad_w1 = s2[28:].reshape(32, 128)[:, :108]
+    grad_w4 = jnp.transpose(s4, (1, 0, 2)).reshape(32, 3456)
     return (activ, grad_w1, grad_w2, grad_w3, grad_w4)
 
 

time: 721 us -> 370 us (0.51)
  waiting for transfers between devices: 403 us -> 98.5 us
  blocking collectives: 105 us -> 28.6 us
  Pallas kernels: 0 us -> 39.1 us
    psum x2 -> x0, waiting for transfers between devices: 374 us -> none  [the longest x1 201 us: per_device(): grad_w4 = lax.psum(local_w4.astype(jnp.bfloat16), 'sx').astype(jnp.float32)]
    psum x1 -> x0, blocking collectives: 78.5 us -> none  [per_device(): lax.psum((local_w1, local_w2, local_w3), ('sx', 'sy', 'ch'))]
    reduce_scatter x1, waiting for transfers between devices: 0.01 us -> 71.3 us  [per_device(): lax.psum_scatter(pieces.astype(jnp.bfloat16), ('sy', 'ch'), scatter_dimen...]
    pallas_call x0 -> x1, Pallas kernels: none -> 39.1 us  [sum_all(): pl.pallas_call(sum_kernel, out_shape=(jax.ShapeDtypeStruct((N3, 64, 128),...]
    unnamed x144 -> x176, local copies, waits for them, and re-layouts: 28.1 us -> 24.4 us
  transfers between devices with their start and end apart: 21 -> 19, of which waited for: 14 -> 13; matrix products, arithmetic and copies ran while one was open for 3% -> 4% of each run, Pallas kernels for 0% -> 0%
where the time goes in v1:
time: 370 us; the launch traced here: 369 us
  waiting for transfers between devices  98.5 us (27%)
  local copies, waits for them, and re-layouts  94.8 us (26%)
  starting transfers between devices  64.5 us (17%)
  Pallas kernels  39.1 us (11%)
  blocking collectives  28.6 us (8%)
  matrix products  22.5 us (6%)
  between operations  15.8 us (4%)
  other arithmetic  5.21 us (1%)
    reduce_scatter x1, waiting for transfers between devices, per_device(): lax.psum_scatter(pieces.astype(jnp.bfloat16), ('sy', 'ch'), scatter_dimen...  71.3 us
    slice x62, local copies, waits for them, and re-layouts, tap_block(): padded[:, depth_tap:depth_tap + stride * (depth - 1) + 1:stride, row_tap:...  45.4 us
    pallas_call x1, Pallas kernels, sum_all(): pl.pallas_call(sum_kernel, out_shape=(jax.ShapeDtypeStruct((N3, 64, 128),...  39.1 us
    all_gather x1, blocking collectives, per_device(): gathered = lax.all_gather(act_three[None], ('sy', 'ch'), axis=0, tiled=True)  28.6 us
    ppermute x6, starting transfers between devices, padded_2(): before = lax.ppermute(last, axis, up)  25.2 us
    unnamed x176, local copies, waits for them, and re-layouts  24.4 us
    ppermute x6, starting transfers between devices, shifted(): return lax.ppermute(value, axis, pairs)  22 us
    ppermute x6, starting transfers between devices, padded_2(): after = lax.ppermute(first, axis, down)  17.2 us
  transfers between devices with their start and end apart: 19, of which 13 were waited for; matrix products, arithmetic and copies ran while one was open for 4% of the time, Pallas kernels for 0%

profile of v1, /device:TPU:1, one launch (start us, length us, event | category | flops | bytes accessed | tf_op | source)
XLA Modules:
  0.0 369.0 jit_solution(5310552448807219401)
XLA Ops:
  8.0 5.7 %collective-permute-start = (bf16[4,1,4,512]{3,0,2,1:T(4,128)(2,1)S(1)}, bf16[4,1,4,512]{3,0,2,1:T(4,128)(2,1)S(1)}, u32[]{:S(2)}, u32[]{:S(2)}) collective-permute-start(bf16[4,1,4,512]{3,0,2,1:T(4,128)(2,1)S(1)} %copy.244), channel_id=1, source_target_pairs={{0,1},{1,8},{8,9},{9,16},{16,17},{17,24},{24,25},{25,32},{32,33},{... | collective-permute-start | bytes 49160 | tf_op jit(solution)/shard_map/ppermute | solution.py:213
  13.6 2.0 collective-permute-done
  16.5 3.1 collective-permute-start.1
  26.3 1.0 slice.887
  27.3 1.0 slice.888
  28.3 1.0 slice.889
  35.0 1.0 slice.877
  36.0 1.0 slice.878
  36.9 1.0 slice.879
  43.6 1.0 slice.897
  44.6 1.0 slice.898
  45.6 1.0 slice.899
  48.8 4.0 %collective-permute-start.2 = (bf16[32,1,2,256]{3,0,2,1:T(8,128)(2,1)S(1)}, bf16[32,1,2,256]{3,0,2,1:T(8,128)(2,1)S(1)}, u32[]{:S(2)}, u32[]{:S(2)}) collective-permute-start(bf16[32,1,2,256]{3,0,2,1:T(8,128)(2,1)S(1)} %slice.1088), channel_id=1, source_target_pairs={{0,1},{1,8},{8,9},{9,16},{16,17},{17,24},{24,25},{25,32},{32,33},{... | collective-permute-start | bytes 98312 | tf_op jit(solution)/shard_map/ppermute | solution.py:213
  52.8 4.1 %collective-permute-done.2 = bf16[32,1,2,256]{3,0,2,1:T(8,128)(2,1)S(1)} collective-permute-done((bf16[32,1,2,256]{3,0,2,1:T(8,128)(2,1)S(1)}, bf16[32,1,2,256]{3,0,2,1:T(8,128)(2,1)S(1)}, u32[]{:S(2)}, u32[]{:S(2)}) %collective-permute-start.2) | collective-permute-done | bytes 32800 | tf_op jit(solution)/shard_map/ppermute | solution.py:213
  57.0 4.1 %collective-permute-start.3 = (bf16[32,3,1,256]{3,0,2,1:T(8,128)(2,1)S(1)}, bf16[32,3,1,256]{3,0,2,1:T(8,128)(2,1)S(1)}, u32[]{:S(2)}, u32[]{:S(2)}) collective-permute-start(bf16[32,3,1,256]{3,0,2,1:T(8,128)(2,1)S(1)} %pad_maximum_fusion.16), channel_id=1, source_target_pairs={{0,2},{2,4},{4,6},{1,3},{3,5},{5,7},{8,10},{10,12},{12,14},{9,11},... | collective-permute-start | bytes 147464 | tf_op jit(solution)/shard_map/ppermute | solution.py:213
  61.1 1.0 collective-permute-done.3
  72.7 3.1 collective-permute-start.4
  75.8 5.4 %collective-permute-start.5 = (bf16[64,1,1,128]{3,0,2,1:T(8,128)(2,1)S(1)}, bf16[64,1,1,128]{3,0,2,1:T(8,128)(2,1)S(1)}, u32[]{:S(2)}, u32[]{:S(2)}) collective-permute-start(bf16[64,1,1,128]{3,0,2,1:T(8,128)(2,1)S(1)} %fusion.140), channel_id=1, source_target_pairs={{1,0},{8,1},{9,8},{16,9},{17,16},{24,17},{25,24},{32,25},{33,32},{... | collective-permute-start | bytes 49160 | tf_op jit(solution)/shard_map/ppermute | solution.py:224
  81.4 3.0 collective-permute-done.5
  84.4 4.0 %collective-permute-start.6 = (bf16[64,3,1,128]{3,0,2,1:T(8,128)(2,1)S(1)}, bf16[64,3,1,128]{3,0,2,1:T(8,128)(2,1)S(1)}, u32[]{:S(2)}, u32[]{:S(2)}) collective-permute-start(bf16[64,3,1,128]{3,0,2,1:T(8,128)(2,1)S(1)} %pad_maximum_fusion.17), channel_id=1, source_target_pairs={{0,2},{2,4},{4,6},{1,3},{3,5},{5,7},{8,10},{10,12},{12,14},{9,11},... | collective-permute-start | bytes 147464 | tf_op jit(solution)/shard_map/ppermute | solution.py:223
  88.4 1.3 collective-permute-start.7
  95.3 28.6 %all-gather = bf16[1024,128]{0,1:T(8,128)(2,1)S(1)} all-gather(bf16[128,128]{0,1:T(8,128)(2,1)S(1)} %get-tuple-element.154), channel_id=2, replica_groups=mesh['sx'=32,'sy'=4,'ch'=2] {'sy','ch'}, dimensions={0}, use_global_device_ids=true | all-gather | bytes 294912 | tf_op jit(solution)/shard_map/all_gather | solution.py:381
  124.2 9.3 %collective-permute-start.8 = (bf16[128,1,4,128]{3,0,2,1:T(8,128)(2,1)S(1)}, bf16[128,1,4,128]{3,0,2,1:T(8,128)(2,1)S(1)}, u32[]{:S(2)}, u32[]{:S(2)}) collective-permute-start(bf16[128,1,4,128]{3,0,2,1:T(8,128)(2,1)S(1)} %get-tuple-element.102), channel_id=1, source_target_pairs={{0,8},{8,16},{16,24},{24,32},{32,40},{40,48},{48,56},{56,64},{64,7... | collective-permute-start | bytes 393224 | tf_op jit(solution)/shard_map/ppermute | solution.py:223
  133.5 2.1 collective-permute-start.9
  136.4 3.5 collective-permute-done.9
  141.3 1.2 constant_dynamic-update-slice_fusion.152
  142.5 1.3 constant_dynamic-update-slice_fusion.151
  143.8 1.2 constant_dynamic-update-slice_fusion.150
  146.5 1.1 constant_dynamic-update-slice_fusion.148
  148.4 1.2 constant_dynamic-update-slice_fusion.147
  149.6 1.2 constant_dynamic-update-slice_fusion.146
  150.8 2.1 constant_dynamic-update-slice_fusion.145
  152.9 1.1 copy.176
  154.8 1.8 copy.177
  156.6 1.8 copy.178
  158.4 1.8 copy.179
  160.2 1.8 copy.181
  163.9 4.4 %copy.175 = bf16[1152,2,4,128]{0,3,2,1:T(8,128)(2,1)} copy(bf16[1152,2,4,128]{3,0,2,1:T(8,128)(2,1)} %get-tuple-element.21) | data formatting | bytes 4718592 | tf_op jit(solution)/shard_map/concatenate | solution.py:251
  168.2 3.1 fusion.94
  172.2 3.0 copy.185
  175.3 1.8 constant_dynamic-update-slice_fusion.72
  177.1 1.7 constant_dynamic-update-slice_fusion.71
  178.8 1.7 constant_dynamic-update-slice_fusion.70
  181.3 1.7 constant_dynamic-update-slice_fusion.68
  185.3 2.5 convolution_add_fusion.3
  189.5 1.9 collective-permute-start.10
  191.4 2.7 collective-permute-start.11
  194.1 2.4 fusion.14
  200.4 1.5 reshape.279
  202.0 1.5 reshape.280
  205.5 2.5 fusion.13
  208.1 2.5 fusion.12
  210.7 71.3 %reduce-scatter.2.cloned.1.call-done = bf16[1,128,1,1,128]{1,4,3,2,0:T(8,128)(2,1)} async-done(((bf16[8,128,1,1,128]{1,4,3,2,0:T(8,128)(2,1)}), bf16[1,128,1,1,128]{1,4,3,2,0:T(8,128)(2,1)}) %reduce-scatter.2.cloned.1.call-update) | async-done | bytes 32784 | tf_op jit(solution)/shard_map/reduce_scatter | solution.py:395
  282.8 4.0 %collective-permute-start.12 = (bf16[128,1,1,128]{0,3,2,1:T(8,128)(2,1)S(1)}, bf16[128,1,1,128]{0,3,2,1:T(8,128)(2,1)S(1)}, u32[]{:S(2)}, u32[]{:S(2)}) collective-permute-start(bf16[128,1,1,128]{0,3,2,1:T(8,128)(2,1)S(1)} %bitcast.346), channel_id=1, source_target_pairs={{0,1},{1,8},{8,9},{9,16},{16,17},{17,24},{24,25},{25,32},{32,33},{... | collective-permute-start | bytes 98312 | tf_op jit(solution)/shard_map/ppermute | solution.py:223
  286.8 4.4 %collective-permute-start.13 = (bf16[128,1,1,128]{0,3,2,1:T(8,128)(2,1)S(1)}, bf16[128,1,1,128]{0,3,2,1:T(8,128)(2,1)S(1)}, u32[]{:S(2)}, u32[]{:S(2)}) collective-permute-start(bf16[128,1,1,128]{0,3,2,1:T(8,128)(2,1)S(1)} %bitcast.347), channel_id=1, source_target_pairs={{1,0},{8,1},{9,8},{16,9},{17,16},{24,17},{25,24},{32,25},{33,32},{... | collective-permute-start | bytes 98312 | tf_op jit(solution)/shard_map/ppermute | solution.py:224
  291.8 2.5 collective-permute-done.13
  294.3 3.0 collective-permute-start.14
  297.3 1.3 collective-permute-start.15
  298.9 3.7 %collective-permute-done.15 = bf16[128,3,1,128]{0,3,2,1:T(8,128)(2,1)S(1)} collective-permute-done((bf16[128,3,1,128]{0,3,2,1:T(8,128)(2,1)S(1)}, bf16[128,3,1,128]{0,3,2,1:T(8,128)(2,1)S(1)}, u32[]{:S(2)}, u32[]{:S(2)}) %collective-permute-start.15) | collective-permute-done | bytes 98336 | tf_op jit(solution)/shard_map/ppermute | solution.py:224
  304.6 3.9 %collective-permute-start.16 = (bf16[64,1,1,128]{3,0,2,1:T(8,128)(2,1)S(1)}, bf16[64,1,1,128]{3,0,2,1:T(8,128)(2,1)S(1)}, u32[]{:S(2)}, u32[]{:S(2)}) collective-permute-start(bf16[64,1,1,128]{3,0,2,1:T(8,128)(2,1)S(1)} %bitcast.343), channel_id=1, source_target_pairs={{1,0},{8,1},{9,8},{16,9},{17,16},{24,17},{25,24},{32,25},{33,32},{... | collective-permute-start | bytes 49160 | tf_op jit(solution)/shard_map/ppermute | solution.py:213
  309.3 2.9 collective-permute-done.16
  312.2 1.3 collective-permute-start.17
  313.8 3.1 collective-permute-done.17
  319.8 39.1 %sum_filter_gradients.1 = (f32[27,64,128]{2,1,0:T(8,128)S(1)}, f32[30,16,128]{2,1,0:T(8,128)S(1)}, f32[27,32,128]{2,1,0:T(8,128)S(1)}) custom-call(bf16[27,64,128]{2,1,0:T(8,128)(2,1)S(1)} %maximum_bitcast_fusion.a3, bf16[30,16,128]{2,1,0:T(8,128)(2,1)S(1)} %pad_maximum_fusion.2.a2, bf16[27,32,128]{2,1,0:T(8,128)(2,1)S(1)} %maximum_bitcast_fusion.1.a4), custom_call_target="tpu_custom_call" | custom-call | tf_op jit(solution)/shard_map/sum_filter_gradients/pallas_call | solution.py:180
  (335 shorter events, 67.2 us)
Async XLA Ops:
  7.2 41.0 %copy-start.30 = (bf16[32,108]{1,0:T(8,128)(2,1)S(1)}, bf16[32,108]{1,0:T(8,128)(2,1)}, u32[]{:S(2)}) copy-start(bf16[32,108]{1,0:T(8,128)(2,1)} %param.7) | copy-start | bytes 20740
  7.2 274.8 %reduce-scatter.2.cloned.1.call-start = ((), (), s32[]{:S(2)}) async-start(), calls=%async_computation.1 | async-start | bytes 294912 | tf_op jit(solution)/shard_map/reduce_scatter | solution.py:395
  8.0 7.6 %collective-permute-start = (bf16[4,1,4,512]{3,0,2,1:T(4,128)(2,1)S(1)}, bf16[4,1,4,512]{3,0,2,1:T(4,128)(2,1)S(1)}, u32[]{:S(2)}, u32[]{:S(2)}) collective-permute-start(bf16[4,1,4,512]{3,0,2,1:T(4,128)(2,1)S(1)} %copy.244), channel_id=1, source_target_pairs={{0,1},{1,8},{8,9},{9,16},{16,17},{17,24},{24,25},{25,32},{32,33},{... | collective-permute-start | bytes 49160 | tf_op jit(solution)/shard_map/ppermute | solution.py:213
  16.5 4.0 %collective-permute-start.1 = (bf16[4,5,1,512]{3,0,2,1:T(4,128)(2,1)S(1)}, bf16[4,5,1,512]{3,0,2,1:T(4,128)(2,1)S(1)}, u32[]{:S(2)}, u32[]{:S(2)}) collective-permute-start(bf16[4,5,1,512]{3,0,2,1:T(4,128)(2,1)S(1)} %slice.1087), channel_id=1, source_target_pairs={{0,2},{2,4},{4,6},{1,3},{3,5},{5,7},{8,10},{10,12},{12,14},{9,11},... | collective-permute-start | bytes 61448 | tf_op jit(solution)/shard_map/ppermute | solution.py:213
  20.7 51.4 %copy-start.17 = (bf16[64,864]{1,0:T(8,128)(2,1)S(1)}, bf16[64,864]{1,0:T(8,128)(2,1)}, u32[]{:S(2)}) copy-start(bf16[64,864]{1,0:T(8,128)(2,1)} %param.8) | copy-start | bytes 331780
  47.0 14.1 %copy-start.7 = (bf16[36,2,2,256]{3,0,2,1:T(8,128)(2,1)}, bf16[36,2,2,256]{3,0,2,1:T(8,128)(2,1)S(1)}, u32[]{:S(2)}) copy-start(bf16[36,2,2,256]{3,0,2,1:T(8,128)(2,1)S(1)} %concatenate.206) | copy-start | bytes 221188
  47.1 43.2 %copy-start.5 = (bf16[32,3456]{1,0:T(8,128)(2,1)S(1)}, bf16[32,3456]{1,0:T(8,128)(2,1)}, u32[]{:S(2)}) copy-start(bf16[32,3456]{1,0:T(8,128)(2,1)} %param.10) | copy-start | bytes 663556
  47.2 13.9 %copy-start.9 = (bf16[36,2,2,256]{3,0,2,1:T(8,128)(2,1)}, bf16[36,2,2,256]{3,0,2,1:T(8,128)(2,1)S(1)}, u32[]{:S(2)}) copy-start(bf16[36,2,2,256]{3,0,2,1:T(8,128)(2,1)S(1)} %concatenate.208) | copy-start | bytes 221188
  48.6 42.9 %copy-start = (bf16[128,1728]{0,1:T(8,128)(2,1)S(1)}, bf16[128,1728]{0,1:T(8,128)(2,1)}, u32[]{:S(2)}) copy-start(bf16[128,1728]{0,1:T(8,128)(2,1)} %param.9) | copy-start | bytes 1327108
  48.8 8.2 %collective-permute-start.2 = (bf16[32,1,2,256]{3,0,2,1:T(8,128)(2,1)S(1)}, bf16[32,1,2,256]{3,0,2,1:T(8,128)(2,1)S(1)}, u32[]{:S(2)}, u32[]{:S(2)}) collective-permute-start(bf16[32,1,2,256]{3,0,2,1:T(8,128)(2,1)S(1)} %slice.1088), channel_id=1, source_target_pairs={{0,1},{1,8},{8,9},{9,16},{16,17},{17,24},{24,25},{25,32},{32,33},{... | collective-permute-start | bytes 98312 | tf_op jit(solution)/shard_map/ppermute | solution.py:213
  57.0 5.1 %collective-permute-start.3 = (bf16[32,3,1,256]{3,0,2,1:T(8,128)(2,1)S(1)}, bf16[32,3,1,256]{3,0,2,1:T(8,128)(2,1)S(1)}, u32[]{:S(2)}, u32[]{:S(2)}) collective-permute-start(bf16[32,3,1,256]{3,0,2,1:T(8,128)(2,1)S(1)} %pad_maximum_fusion.16), channel_id=1, source_target_pairs={{0,2},{2,4},{4,6},{1,3},{3,5},{5,7},{8,10},{10,12},{12,14},{9,11},... | collective-permute-start | bytes 147464 | tf_op jit(solution)/shard_map/ppermute | solution.py:213
  71.9 20.4 %copy-start.23 = (bf16[288,1,1,128]{3,0,2,1:T(8,128)(2,1)}, bf16[288,1,1,128]{3,0,2,1:T(8,128)(2,1)S(1)}, u32[]{:S(2)}) copy-start(bf16[288,1,1,128]{3,0,2,1:T(8,128)(2,1)S(1)} %constant_dynamic-update-slice_fusion.20) | copy-start | bytes 221188
  72.0 20.3 %copy-start.21 = (bf16[288,1,1,128]{3,0,2,1:T(8,128)(2,1)}, bf16[288,1,1,128]{3,0,2,1:T(8,128)(2,1)S(1)}, u32[]{:S(2)}) copy-start(bf16[288,1,1,128]{3,0,2,1:T(8,128)(2,1)S(1)} %constant_dynamic-update-slice_fusion.11) | copy-start | bytes 221188
  72.1 20.2 %copy-start.19 = (bf16[288,1,1,128]{3,0,2,1:T(8,128)(2,1)}, bf16[288,1,1,128]{3,0,2,1:T(8,128)(2,1)S(1)}, u32[]{:S(2)}) copy-start(bf16[288,1,1,128]{3,0,2,1:T(8,128)(2,1)S(1)} %constant_dynamic-update-slice_fusion.2) | copy-start | bytes 221188
  72.7 20.9 %copy-start.25 = (f32[64,128]{1,0:T(8,128)}, f32[64,128]{1,0:T(8,128)S(1)}, u32[]{:S(2)}) copy-start(f32[64,128]{1,0:T(8,128)S(1)} %fusion.16) | copy-start | bytes 98308
  72.7 8.7 %collective-permute-start.4 = (bf16[64,1,1,128]{3,0,2,1:T(8,128)(2,1)S(1)}, bf16[64,1,1,128]{3,0,2,1:T(8,128)(2,1)S(1)}, u32[]{:S(2)}, u32[]{:S(2)}) collective-permute-start(bf16[64,1,1,128]{3,0,2,1:T(8,128)(2,1)S(1)} %fusion.140), channel_id=1, source_target_pairs={{0,1},{1,8},{8,9},{9,16},{16,17},{17,24},{24,25},{25,32},{32,33},{... | collective-permute-start | bytes 49160 | tf_op jit(solution)/shard_map/ppermute | solution.py:223
  75.8 8.6 %collective-permute-start.5 = (bf16[64,1,1,128]{3,0,2,1:T(8,128)(2,1)S(1)}, bf16[64,1,1,128]{3,0,2,1:T(8,128)(2,1)S(1)}, u32[]{:S(2)}, u32[]{:S(2)}) collective-permute-start(bf16[64,1,1,128]{3,0,2,1:T(8,128)(2,1)S(1)} %fusion.140), channel_id=1, source_target_pairs={{1,0},{8,1},{9,8},{16,9},{17,16},{24,17},{25,24},{32,25},{33,32},{... | collective-permute-start | bytes 49160 | tf_op jit(solution)/shard_map/ppermute | solution.py:224
  81.4 54.3 %copy-start.3 = (bf16[64,864]{0,1:T(8,128)(2,1)}, bf16[64,864]{0,1:T(8,128)(2,1)S(1)}, u32[]{:S(2)}) copy-start(bf16[64,864]{0,1:T(8,128)(2,1)S(1)} %copy.193) | copy-start | bytes 331780
  84.4 8.8 %collective-permute-start.6 = (bf16[64,3,1,128]{3,0,2,1:T(8,128)(2,1)S(1)}, bf16[64,3,1,128]{3,0,2,1:T(8,128)(2,1)S(1)}, u32[]{:S(2)}, u32[]{:S(2)}) collective-permute-start(bf16[64,3,1,128]{3,0,2,1:T(8,128)(2,1)S(1)} %pad_maximum_fusion.17), channel_id=1, source_target_pairs={{0,2},{2,4},{4,6},{1,3},{3,5},{5,7},{8,10},{10,12},{12,14},{9,11},... | collective-permute-start | bytes 147464 | tf_op jit(solution)/shard_map/ppermute | solution.py:223
  88.4 4.9 %collective-permute-start.7 = (bf16[64,3,1,128]{3,0,2,1:T(8,128)(2,1)S(1)}, bf16[64,3,1,128]{3,0,2,1:T(8,128)(2,1)S(1)}, u32[]{:S(2)}, u32[]{:S(2)}) collective-permute-start(bf16[64,3,1,128]{3,0,2,1:T(8,128)(2,1)S(1)} %pad_maximum_fusion.17), channel_id=1, source_target_pairs={{2,0},{4,2},{6,4},{3,1},{5,3},{7,5},{10,8},{12,10},{14,12},{11,9},... | collective-permute-start | bytes 147464 | tf_op jit(solution)/shard_map/ppermute | solution.py:224
  93.9 41.8 %copy-start.27 = (bf16[576,1,1,128]{3,0,2,1:T(8,128)(2,1)}, bf16[576,1,1,128]{3,0,2,1:T(8,128)(2,1)S(1)}, u32[]{:S(2)}) copy-start(bf16[576,1,1,128]{3,0,2,1:T(8,128)(2,1)S(1)} %get-tuple-element.84) | copy-start | bytes 442372
  93.9 46.5 %copy-start.13 = (bf16[576,1,1,128]{3,0,2,1:T(8,128)(2,1)}, bf16[576,1,1,128]{3,0,2,1:T(8,128)(2,1)S(1)}, u32[]{:S(2)}) copy-start(bf16[576,1,1,128]{3,0,2,1:T(8,128)(2,1)S(1)} %get-tuple-element.85) | copy-start | bytes 442372
  93.9 46.5 %copy-start.15 = (bf16[576,1,1,128]{3,0,2,1:T(8,128)(2,1)}, bf16[576,1,1,128]{3,0,2,1:T(8,128)(2,1)S(1)}, u32[]{:S(2)}) copy-start(bf16[576,1,1,128]{3,0,2,1:T(8,128)(2,1)S(1)} %get-tuple-element.86) | copy-start | bytes 442372
  124.2 12.1 %collective-permute-start.8 = (bf16[128,1,4,128]{3,0,2,1:T(8,128)(2,1)S(1)}, bf16[128,1,4,128]{3,0,2,1:T(8,128)(2,1)S(1)}, u32[]{:S(2)}, u32[]{:S(2)}) collective-permute-start(bf16[128,1,4,128]{3,0,2,1:T(8,128)(2,1)S(1)} %get-tuple-element.102), channel_id=1, source_target_pairs={{0,8},{8,16},{16,24},{24,32},{32,40},{40,48},{48,56},{56,64},{64,7... | collective-permute-start | bytes 393224 | tf_op jit(solution)/shard_map/ppermute | solution.py:223
  133.5 6.3 %collective-permute-start.9 = (bf16[128,1,4,128]{3,0,2,1:T(8,128)(2,1)S(1)}, bf16[128,1,4,128]{3,0,2,1:T(8,128)(2,1)S(1)}, u32[]{:S(2)}, u32[]{:S(2)}) collective-permute-start(bf16[128,1,4,128]{3,0,2,1:T(8,128)(2,1)S(1)} %get-tuple-element.103), channel_id=1, source_target_pairs={{8,0},{16,8},{24,16},{32,24},{40,32},{48,40},{56,48},{64,56},{72,6... | collective-permute-start | bytes 393224 | tf_op jit(solution)/shard_map/ppermute | solution.py:224
  175.3 7.7 %copy-start.2 = (bf16[128,2,4,128]{0,3,2,1:T(8,128)(2,1)S(1)}, bf16[128,2,4,128]{0,3,2,1:T(8,128)(2,1)}, u32[]{:S(2)}) copy-start(bf16[128,2,4,128]{0,3,2,1:T(8,128)(2,1)} %copy.182) | copy-start | bytes 786436
  175.3 8.5 %copy-start.1 = (bf16[128,2,4,128]{0,3,2,1:T(8,128)(2,1)S(1)}, bf16[128,2,4,128]{0,3,2,1:T(8,128)(2,1)}, u32[]{:S(2)}) copy-start(bf16[128,2,4,128]{0,3,2,1:T(8,128)(2,1)} %copy.183) | copy-start | bytes 786436
  175.3 10.0 %copy-start.6 = (bf16[32,3456]{1,0:T(8,128)(2,1)S(1)}, bf16[32,3456]{1,0:T(8,128)(2,1)}, u32[]{:S(2)}) copy-start(bf16[32,3456]{1,0:T(8,128)(2,1)} %param.10) | copy-start | bytes 663556
  175.3 10.0 %copy-start.18 = (f32[1024,32]{0,1:T(8,128)S(1)}, f32[1024,32]{0,1:T(8,128)}, u32[]{:S(2)}) copy-start(f32[1024,32]{0,1:T(8,128)} %fusion.94) | copy-start | bytes 393220
  189.5 7.1 %collective-permute-start.10 = (bf16[32,1,4,128]{3,2,1,0:T(4,128)(2,1)S(1)}, bf16[32,1,4,128]{3,2,1,0:T(4,128)(2,1)S(1)}, u32[]{:S(2)}, u32[]{:S(2)}) collective-permute-start(bf16[32,1,4,128]{3,2,1,0:T(4,128)(2,1)S(1)} %get-tuple-element.144), channel_id=1, source_target_pairs={{0,8},{8,16},{16,24},{24,32},{32,40},{40,48},{48,56},{56,64},{64,7... | collective-permute-start | bytes 98312 | tf_op jit(solution)/shard_map/ppermute | solution.py:223
  191.4 5.5 %collective-permute-start.11 = (bf16[32,1,4,128]{3,2,1,0:T(4,128)(2,1)S(1)}, bf16[32,1,4,128]{3,2,1,0:T(4,128)(2,1)S(1)}, u32[]{:S(2)}, u32[]{:S(2)}) collective-permute-start(bf16[32,1,4,128]{3,2,1,0:T(4,128)(2,1)S(1)} %get-tuple-element.145), channel_id=1, source_target_pairs={{8,0},{16,8},{24,16},{32,24},{40,32},{48,40},{56,48},{64,56},{72,6... | collective-permute-start | bytes 98312 | tf_op jit(solution)/shard_map/ppermute | solution.py:224
  205.5 76.5 %copy-start.32 = (f32[128,128]{0,1:T(8,128)S(1)}, f32[128,128]{0,1:T(8,128)}, u32[]{:S(2)}) copy-start(f32[128,128]{0,1:T(8,128)} %get-tuple-element.155) | copy-start | bytes 196612
  205.5 85.7 %copy-start.16 = (bf16[576,1,1,128]{3,0,2,1:T(8,128)(2,1)S(1)}, bf16[576,1,1,128]{3,0,2,1:T(8,128)(2,1)}, u32[]{:S(2)}) copy-start(bf16[576,1,1,128]{3,0,2,1:T(8,128)(2,1)} %copy-done.15) | copy-start | bytes 442372
  208.0 83.4 %copy-start.14 = (bf16[576,1,1,128]{3,0,2,1:T(8,128)(2,1)S(1)}, bf16[576,1,1,128]{3,0,2,1:T(8,128)(2,1)}, u32[]{:S(2)}) copy-start(bf16[576,1,1,128]{3,0,2,1:T(8,128)(2,1)} %copy-done.13) | copy-start | bytes 442372
  208.1 83.5 %copy-start.28 = (bf16[576,1,1,128]{3,0,2,1:T(8,128)(2,1)S(1)}, bf16[576,1,1,128]{3,0,2,1:T(8,128)(2,1)}, u32[]{:S(2)}) copy-start(bf16[576,1,1,128]{3,0,2,1:T(8,128)(2,1)} %copy-done.27) | copy-start | bytes 442372
  282.8 9.0 %collective-permute-start.12 = (bf16[128,1,1,128]{0,3,2,1:T(8,128)(2,1)S(1)}, bf16[128,1,1,128]{0,3,2,1:T(8,128)(2,1)S(1)}, u32[]{:S(2)}, u32[]{:S(2)}) collective-permute-start(bf16[128,1,1,128]{0,3,2,1:T(8,128)(2,1)S(1)} %bitcast.346), channel_id=1, source_target_pairs={{0,1},{1,8},{8,9},{9,16},{16,17},{17,24},{24,25},{25,32},{32,33},{... | collective-permute-start | bytes 98312 | tf_op jit(solution)/shard_map/ppermute | solution.py:223
  286.8 7.5 %collective-permute-start.13 = (bf16[128,1,1,128]{0,3,2,1:T(8,128)(2,1)S(1)}, bf16[128,1,1,128]{0,3,2,1:T(8,128)(2,1)S(1)}, u32[]{:S(2)}, u32[]{:S(2)}) collective-permute-start(bf16[128,1,1,128]{0,3,2,1:T(8,128)(2,1)S(1)} %bitcast.347), channel_id=1, source_target_pairs={{1,0},{8,1},{9,8},{16,9},{17,16},{24,17},{25,24},{32,25},{33,32},{... | collective-permute-start | bytes 98312 | tf_op jit(solution)/shard_map/ppermute | solution.py:224
  291.6 12.2 %copy-start.26 = (f32[64,128]{1,0:T(8,128)S(1)}, f32[64,128]{1,0:T(8,128)}, u32[]{:S(2)}) copy-start(f32[64,128]{1,0:T(8,128)} %copy-done.25) | copy-start | bytes 98308
  294.3 9.7 %copy-start.22 = (bf16[288,1,1,128]{3,0,2,1:T(8,128)(2,1)S(1)}, bf16[288,1,1,128]{3,0,2,1:T(8,128)(2,1)}, u32[]{:S(2)}) copy-start(bf16[288,1,1,128]{3,0,2,1:T(8,128)(2,1)} %copy-done.21) | copy-start | bytes 221188
  294.3 9.9 %copy-start.24 = (bf16[288,1,1,128]{3,0,2,1:T(8,128)(2,1)S(1)}, bf16[288,1,1,128]{3,0,2,1:T(8,128)(2,1)}, u32[]{:S(2)}) copy-start(bf16[288,1,1,128]{3,0,2,1:T(8,128)(2,1)} %copy-done.23) | copy-start | bytes 221188
  294.3 4.6 %collective-permute-start.14 = (bf16[128,3,1,128]{0,3,2,1:T(8,128)(2,1)S(1)}, bf16[128,3,1,128]{0,3,2,1:T(8,128)(2,1)S(1)}, u32[]{:S(2)}, u32[]{:S(2)}) collective-permute-start(bf16[128,3,1,128]{0,3,2,1:T(8,128)(2,1)S(1)} %pad_maximum_fusion.6), channel_id=1, source_target_pairs={{0,2},{2,4},{4,6},{1,3},{3,5},{5,7},{8,10},{10,12},{12,14},{9,11},... | collective-permute-start | bytes 294920 | tf_op jit(solution)/shard_map/ppermute | solution.py:223
  297.3 5.4 %collective-permute-start.15 = (bf16[128,3,1,128]{0,3,2,1:T(8,128)(2,1)S(1)}, bf16[128,3,1,128]{0,3,2,1:T(8,128)(2,1)S(1)}, u32[]{:S(2)}, u32[]{:S(2)}) collective-permute-start(bf16[128,3,1,128]{0,3,2,1:T(8,128)(2,1)S(1)} %pad_maximum_fusion.6), channel_id=1, source_target_pairs={{2,0},{4,2},{6,4},{3,1},{5,3},{7,5},{10,8},{12,10},{14,12},{11,9},... | collective-permute-start | bytes 294920 | tf_op jit(solution)/shard_map/ppermute | solution.py:224
  298.7 5.7 %copy-start.20 = (bf16[288,1,1,128]{3,0,2,1:T(8,128)(2,1)S(1)}, bf16[288,1,1,128]{3,0,2,1:T(8,128)(2,1)}, u32[]{:S(2)}) copy-start(bf16[288,1,1,128]{3,0,2,1:T(8,128)(2,1)} %copy-done.19) | copy-start | bytes 221188
  302.9 14.4 %copy-start.33 = (bf16[64,32]{0,1:T(8,128)(2,1)S(1)}, bf16[64,32]{0,1:T(8,128)(2,1)}, u32[]{:S(2)}) copy-start(bf16[64,32]{0,1:T(8,128)(2,1)} %get-tuple-element.128) | copy-start | bytes 12292
  302.9 14.4 %copy-start.34 = (bf16[64,32]{0,1:T(8,128)(2,1)S(1)}, bf16[64,32]{0,1:T(8,128)(2,1)}, u32[]{:S(2)}) copy-start(bf16[64,32]{0,1:T(8,128)(2,1)} %get-tuple-element.129) | copy-start | bytes 12292
  302.9 14.8 %copy-start.37 = (bf16[64,32]{0,1:T(8,128)(2,1)S(1)}, bf16[64,32]{0,1:T(8,128)(2,1)}, u32[]{:S(2)}) copy-start(bf16[64,32]{0,1:T(8,128)(2,1)} %get-tuple-element.123) | copy-start | bytes 12292
  303.0 14.8 %copy-start.38 = (bf16[64,32]{0,1:T(8,128)(2,1)S(1)}, bf16[64,32]{0,1:T(8,128)(2,1)}, u32[]{:S(2)}) copy-start(bf16[64,32]{0,1:T(8,128)(2,1)} %get-tuple-element.124) | copy-start | bytes 12292
  303.0 14.8 %copy-start.39 = (bf16[64,32]{0,1:T(8,128)(2,1)S(1)}, bf16[64,32]{0,1:T(8,128)(2,1)}, u32[]{:S(2)}) copy-start(bf16[64,32]{0,1:T(8,128)(2,1)} %get-tuple-element.125) | copy-start | bytes 12292
  303.0 14.8 %copy-start.48 = (bf16[64,32]{0,1:T(8,128)(2,1)S(1)}, bf16[64,32]{0,1:T(8,128)(2,1)}, u32[]{:S(2)}) copy-start(bf16[64,32]{0,1:T(8,128)(2,1)} %get-tuple-element.122) | copy-start | bytes 12292
  303.0 14.9 %copy-start.35 = (bf16[64,32]{0,1:T(8,128)(2,1)S(1)}, bf16[64,32]{0,1:T(8,128)(2,1)}, u32[]{:S(2)}) copy-start(bf16[64,32]{0,1:T(8,128)(2,1)} %get-tuple-element.120) | copy-start | bytes 12292
  303.1 14.9 %copy-start.36 = (bf16[64,32]{0,1:T(8,128)(2,1)S(1)}, bf16[64,32]{0,1:T(8,128)(2,1)}, u32[]{:S(2)}) copy-start(bf16[64,32]{0,1:T(8,128)(2,1)} %get-tuple-element.121) | copy-start | bytes 12292
  303.1 15.0 %copy-start.44 = (bf16[64,32]{0,1:T(8,128)(2,1)S(1)}, bf16[64,32]{0,1:T(8,128)(2,1)}, u32[]{:S(2)}) copy-start(bf16[64,32]{0,1:T(8,128)(2,1)} %get-tuple-element.116) | copy-start | bytes 12292
  303.1 15.0 %copy-start.45 = (bf16[64,32]{0,1:T(8,128)(2,1)S(1)}, bf16[64,32]{0,1:T(8,128)(2,1)}, u32[]{:S(2)}) copy-start(bf16[64,32]{0,1:T(8,128)(2,1)} %get-tuple-element.117) | copy-start | bytes 12292
  303.1 15.0 %copy-start.46 = (bf16[64,32]{0,1:T(8,128)(2,1)S(1)}, bf16[64,32]{0,1:T(8,128)(2,1)}, u32[]{:S(2)}) copy-start(bf16[64,32]{0,1:T(8,128)(2,1)} %get-tuple-element.118) | copy-start | bytes 12292
  303.1 15.0 %copy-start.47 = (bf16[64,32]{0,1:T(8,128)(2,1)S(1)}, bf16[64,32]{0,1:T(8,128)(2,1)}, u32[]{:S(2)}) copy-start(bf16[64,32]{0,1:T(8,128)(2,1)} %get-tuple-element.119) | copy-start | bytes 12292
  303.2 15.2 %copy-start.40 = (bf16[64,32]{0,1:T(8,128)(2,1)S(1)}, bf16[64,32]{0,1:T(8,128)(2,1)}, u32[]{:S(2)}) copy-start(bf16[64,32]{0,1:T(8,128)(2,1)} %get-tuple-element.112) | copy-start | bytes 12292
  303.2 15.2 %copy-start.41 = (bf16[64,32]{0,1:T(8,128)(2,1)S(1)}, bf16[64,32]{0,1:T(8,128)(2,1)}, u32[]{:S(2)}) copy-start(bf16[64,32]{0,1:T(8,128)(2,1)} %get-tuple-element.113) | copy-start | bytes 12292
  303.2 15.2 %copy-start.42 = (bf16[64,32]{0,1:T(8,128)(2,1)S(1)}, bf16[64,32]{0,1:T(8,128)(2,1)}, u32[]{:S(2)}) copy-start(bf16[64,32]{0,1:T(8,128)(2,1)} %get-tuple-element.114) | copy-start | bytes 12292
  303.2 15.2 %copy-start.43 = (bf16[64,32]{0,1:T(8,128)(2,1)S(1)}, bf16[64,32]{0,1:T(8,128)(2,1)}, u32[]{:S(2)}) copy-start(bf16[64,32]{0,1:T(8,128)(2,1)} %get-tuple-element.115) | copy-start | bytes 12292
  303.3 15.3 %copy-start.29 = (bf16[512,32]{0,1:T(8,128)(2,1)S(1)}, bf16[512,32]{0,1:T(8,128)(2,1)}, u32[]{:S(2)}) copy-start(bf16[512,32]{0,1:T(8,128)(2,1)} %concatenate.261) | copy-start | bytes 98308
  304.2 15.0 %copy-start.8 = (bf16[36,2,2,256]{3,0,2,1:T(8,128)(2,1)S(1)}, bf16[36,2,2,256]{3,0,2,1:T(8,128)(2,1)}, u32[]{:S(2)}) copy-start(bf16[36,2,2,256]{3,0,2,1:T(8,128)(2,1)} %copy-done.7) | copy-start | bytes 221188
  304.6 15.0 %copy-start.10 = (bf16[36,2,2,256]{3,0,2,1:T(8,128)(2,1)S(1)}, bf16[36,2,2,256]{3,0,2,1:T(8,128)(2,1)}, u32[]{:S(2)}) copy-start(bf16[36,2,2,256]{3,0,2,1:T(8,128)(2,1)} %copy-done.9) | copy-start | bytes 221188
  304.6 7.6 %collective-permute-start.16 = (bf16[64,1,1,128]{3,0,2,1:T(8,128)(2,1)S(1)}, bf16[64,1,1,128]{3,0,2,1:T(8,128)(2,1)S(1)}, u32[]{:S(2)}, u32[]{:S(2)}) collective-permute-start(bf16[64,1,1,128]{3,0,2,1:T(8,128)(2,1)S(1)} %bitcast.343), channel_id=1, source_target_pairs={{1,0},{8,1},{9,8},{16,9},{17,16},{24,17},{25,24},{32,25},{33,32},{... | collective-permute-start | bytes 49160 | tf_op jit(solution)/shard_map/ppermute | solution.py:213
  312.2 4.6 %collective-permute-start.17 = (bf16[64,2,1,128]{3,0,2,1:T(8,128)(2,1)S(1)}, bf16[64,2,1,128]{3,0,2,1:T(8,128)(2,1)S(1)}, u32[]{:S(2)}, u32[]{:S(2)}) collective-permute-start(bf16[64,2,1,128]{3,0,2,1:T(8,128)(2,1)S(1)} %pad_maximum_fusion.24), channel_id=1, source_target_pairs={{2,0},{4,2},{6,4},{3,1},{5,3},{7,5},{10,8},{12,10},{14,12},{11,9},... | collective-permute-start | bytes 98312 | tf_op jit(solution)/shard_map/ppermute | solution.py:213
  (4 other events, 11.2 us)
Sparse Core Ops, SparseCore 0:
  205.6 76.2 reduce-scatter.1

commit v2 on v0

v2 whole, which is shorter than its diff:
```python
import numpy as np
import jax
import jax.numpy as jnp
from jax import lax
from jax.experimental import pallas as pl
from jax.experimental.pallas import tpu as pltpu
from jax.sharding import PartitionSpec as P

MESH = pl.DeviceIdType.MESH
BF = jnp.bfloat16
F32 = jnp.float32
N3, N2, N4 = 27, 30, 27


def row_choice():
    pick = np.zeros((224, 256), np.float32)
    for d in range(7):
        for h in range(7):
            block = (0 if d >= 3 else 1) + (0 if h >= 3 else 2)
            for c in range(4):
                source = block * 64 + c * 16 + ((d + 1) % 4) * 4 + (h + 1) % 4
                pick[d * 32 + h * 4 + c, source] = 1.0
    return pick


def band_choice():
    pick = np.zeros((3, 128, 288), np.float32)
    for j in range(3):
        for kd in range(3):
            for kh in range(3):
                for kw in range(3):
                    for c in range(4):
                        pick[j, (9 * kd + 3 * kh + kw) * 4 + c, kw * 96 + kd * 32 + (2 * j + kh) * 4 + c] = 1.0
    return pick


def smooth_unit(values):
    return 0.3 * values + 0.7 * values * jax.nn.sigmoid(values)


def smooth_slope(values):
    sigma = jax.nn.sigmoid(values)
    return 0.3 + 0.7 * (sigma + values * sigma * (1.0 - sigma))


def mm(a, b):
    return jnp.dot(a, b, preferred_element_type=F32)


def mm_nt(a, b):
    return lax.dot_general(a, b, (((1,), (1,)), ((), ())), preferred_element_type=F32)


def lane_of(shape):
    return lax.broadcasted_iota(jnp.int32, shape, len(shape) - 1)


def from_left(x):
    return jnp.where(lane_of(x.shape) == 0, 0.0, pltpu.roll(x, 1, 1))


def from_right(x):
    return jnp.where(lane_of(x.shape) == 127, 0.0, pltpu.roll(x, 127, 1))


def await_bytes(ref, sem):
    pltpu.make_async_copy(ref, ref, sem).wait()


def whole_kernel(
    vol, w1, w2, w3, w4, gout, rows_pick, band,
    activ, o1, o2, o3, o4,
    perm, w1band, wbk_t, wbk, wb4_t, wb4, w3b,
    vin, vst, p1, a1, gath, x2s, s2own, s2buf, p3, x3s,
    g4send, g4halo, g4s, rs_send, rs_recv, g3own, g3buf, g3s, g2st,
    a3, a2, a4, in3, in2, in4, mid3, mid2, part3, part2, all3, all2, all4,
    send, recv, scale,
):
    sx, sy, ch = lax.axis_index("sx"), lax.axis_index("sy"), lax.axis_index("ch")
    core = lax.rem(sx, 2)
    z = lax.rem(lax.div(sx, 2), 8)
    low = lax.div(sx, 16)
    rank = low * 16 + core * 8 + ch * 4 + sy
    g = sx * 2 + ch
    cell = ch * 4 + sy

    def block_place(depth_block, row_block):
        d = lax.rem(depth_block + 64, 64)
        return (lax.div(d, 2), lax.rem(row_block + 4, 4), lax.rem(d, 2))

    def near(k):
        other = lax.rem(cell + 8 + k, 24)
        group = lax.div(other, 8) - 1
        return group, (lax.rem(sx + group + 32, 32), lax.rem(other, 4), lax.rem(lax.div(other, 4), 2))

    def plane(k):
        other = lax.rem(rank + k, 32)
        place = (
            lax.div(other, 16) * 16 + z * 2 + lax.rem(lax.div(other, 8), 2),
            lax.rem(other, 4),
            lax.rem(lax.div(other, 4), 2),
        )
        return other, place

    def column(k):
        other = lax.rem(z + k, 8)
        return other, (low * 16 + other * 2 + core, sy, ch)

    def depth(k):
        other = lax.rem(sx + k, 32)
        return other, (other, sy, ch)

    def loop(count, step, start=1):
        def body(k, carry):
            step(k)
            return carry
        lax.fori_loop(start, count, body, 0)

    def push(src, dst, slot, place):
        pltpu.make_async_remote_copy(
            src_ref=src, dst_ref=dst, send_sem=send.at[slot], recv_sem=recv.at[slot],
            device_id=place, device_id_type=MESH,
        ).start()

    barrier = pltpu.get_barrier_semaphore()

    def greet(count, where):
        def step(k):
            pl.semaphore_signal(barrier, inc=1, device_id=where(k)[1], device_id_type=MESH)
        loop(count, step)

    greet(24, near)
    greet(32, plane)
    greet(8, column)
    greet(32, depth)

    for p in range(4):
        r = lax.broadcasted_iota(jnp.int32, (512, 128), 0)
        perm[:, p * 128 : (p + 1) * 128] = jnp.where(r == 4 * lane_of((512, 128)) + p, 1.0, 0.0).astype(BF)
    for j in range(3):
        w1band[j * 32 : (j + 1) * 32, :] = mm(w1[...], band[j, :108, :]).astype(BF)
    pl.semaphore_wait(barrier, 23 + 31 + 7 + 31)

    push(vol, vin.at[0], 0, block_place(g + 1, sy))
    push(vol, vin.at[1], 0, block_place(g, sy + 1))
    push(vol, vin.at[2], 0, block_place(g + 1, sy + 1))

    zero = jnp.zeros((96, 128), BF)
    for d in range(6):
        for h in (0, 5):
            at = (d * 6 + h) * 128
            for r in range(2):
                x2s[r * 96 : (r + 1) * 96, at : at + 128] = zero
            if d < 4:
                g4s[:, at : at + 128] = zero
                for r in range(4):
                    x3s[r * 96 : (r + 1) * 96, at : at + 128] = zero
    for t in range(27):
        wb4_t[t * 32 : (t + 1) * 32, :] = w4[:, (26 - t) * 128 : (27 - t) * 128]
    wb4_t[864:896, :] = jnp.zeros((32, 128), BF)
    for k in range(7):
        wb4[:, k * 128 : (k + 1) * 128] = wb4_t[k * 128 : (k + 1) * 128, :].astype(F32).T.astype(BF)
    for k in range(14):
        if k < 13:
            turned = w3[:, k * 128 : (k + 1) * 128].astype(F32).T.astype(BF)
        else:
            turned = w3[:, 1664:1728].astype(F32).T.astype(BF)
        w3b[:, (26 - 2 * k) * 128 : (27 - 2 * k) * 128] = turned[:64]
        if k < 13:
            w3b[:, (25 - 2 * k) * 128 : (26 - 2 * k) * 128] = turned[64:]
    wbk_t[...] = jnp.zeros((512, 256), BF)
    taps = {(0, 0): 1, (1, 0): 2, (1, 1): 0}
    for (pa, a), kd in taps.items():
        for (pb, b), kh in taps.items():
            for (pe, s), kw in taps.items():
                r = (a * 4 + b * 2 + s) * 64
                c = (pa * 4 + pe * 2 + pb) * 32
                t = (9 * kd + 3 * kh + kw) * 32
                wbk_t[r : r + 64, c : c + 32] = w2[:, t : t + 32]
    for r in range(4):
        for c in range(2):
            block = wbk_t[r * 128 : (r + 1) * 128, c * 128 : (c + 1) * 128]
            wbk[c * 128 : (c + 1) * 128, r * 128 : (r + 1) * 128] = block.astype(F32).T.astype(BF)

    await_bytes(vin, recv.at[0])
    none = jnp.zeros((64, 512), BF)
    blocks = jnp.concatenate(
        [
            vol[...],
            jnp.where(g > 0, vin[0], none),
            jnp.where(sy > 0, vin[1], none),
            jnp.where((g > 0) & (sy > 0), vin[2], none),
        ],
        axis=0,
    )
    ordered = mm(mm(rows_pick[...], blocks).astype(BF), perm[...])
    phases = [ordered[:, p * 128 : (p + 1) * 128] for p in range(4)]
    before = from_left(phases[3]).astype(BF)
    phases = [x.astype(BF) for x in phases]
    for q, used in enumerate(((before, phases[0], phases[1]), (phases[1], phases[2], phases[3]))):
        for kw in range(3):
            for i in range(3):
                at = (2 * i + q) * 128
                vst[kw * 96 : (kw + 1) * 96, at : at + 128] = used[kw][64 * i : 64 * i + 96]
    pre_one = mm(w1band[...], vst[...])
    p1[...] = pre_one[32:, 256:]
    act_one = smooth_unit(pre_one)
    for i in range(3):
        even = act_one[:, (2 * i) * 128 : (2 * i + 1) * 128]
        odd = act_one[:, (2 * i + 1) * 128 : (2 * i + 2) * 128]
        three = (from_left(odd).astype(BF), even.astype(BF), odd.astype(BF))
        for j in range(3):
            for kw in range(3):
                r = (3 * i + j) * 96 + kw * 32
                a1[r : r + 32, :] = three[kw][j * 32 : (j + 1) * 32]
    pre_two = mm(w2[...], a1[...])
    act_two = smooth_unit(pre_two).astype(BF)
    own = (ch + 2) * 4 + sy
    gath[own] = act_two

    def send_act(k):
        group, place = near(k)
        push(gath.at[own], gath.at[own - 8 * group], 1, place)
    loop(24, send_act)
    slope_two = smooth_slope(pre_two)
    s2own[...] = slope_two
    s2buf[0] = slope_two
    push(s2own, s2buf.at[1], 2, block_place(g, sy - 1))
    push(s2own, s2buf.at[2], 2, block_place(g - 1, sy))
    push(s2own, s2buf.at[3], 2, block_place(g - 1, sy - 1))
    await_bytes(gath.at[pl.ds(0, 23)], recv.at[1])

    def spread_three(ref, rows, at, x, keep):
        if keep is not None:
            x = jnp.where(keep, x, 0.0)
        ref[0:rows, pl.ds(at, 128)] = from_left(x).astype(BF)
        ref[rows : 2 * rows, pl.ds(at, 128)] = x.astype(BF)
        ref[2 * rows : 3 * rows, pl.ds(at, 128)] = from_right(x).astype(BF)

    for d in range(6):
        keep = sx > 0 if d < 2 else (sx < 31 if d > 3 else None)
        for h in range(4):
            spread_three(x2s, 64, (d * 6 + h + 1) * 128, gath[d * 4 + h].astype(F32), keep)

    def taps_of(ref, p):
        return jnp.concatenate(
            [ref[:, ((p + kd) * 6 + kh) * 128 : ((p + kd) * 6 + kh + 4) * 128] for kd in range(3) for kh in range(3)],
            axis=0,
        )

    for p in range(4):
        pre = mm(w3[...], taps_of(x2s, p))
        act = smooth_unit(pre)
        keep = sx > 0 if p == 0 else (sx < 31 if p == 3 else None)
        for h in range(4):
            piece = slice(h * 128, (h + 1) * 128)
            if p in (1, 2):
                p3[(p - 1) * 4 + h] = pre[:, piece]
            spread_three(x3s, 128, (p * 6 + h + 1) * 128, act[:, piece].astype(BF).astype(F32), keep)

    grads = []
    for p in range(2):
        pre = mm(w4[...], taps_of(x3s, p))
        here = slice(p * 512, (p + 1) * 512)
        activ[:, here] = smooth_unit(pre).astype(BF)
        grad = (gout[:, here].astype(F32) * smooth_slope(pre) * scale).astype(BF)
        grads.append(grad)
        g4send[p] = grad
    push(g4send.at[0], g4halo.at[1], 3, (lax.rem(sx + 31, 32), sy, ch))
    push(g4send.at[1], g4halo.at[0], 3, (lax.rem(sx + 1, 32), sy, ch))
    for kd in range(3):
        for kh in range(3):
            part = None
            for p in range(2):
                at = ((p + kd) * 6 + kh) * 128
                more = mm_nt(grads[p], x3s[:, at : at + 512])
                part = more if part is None else part + more
            for kw in range(3):
                a4[9 * kd + 3 * kh + kw] = part[:, kw * 128 : (kw + 1) * 128].astype(BF)
    for p in range(2):
        for h in range(4):
            x = grads[p][:, h * 128 : (h + 1) * 128].astype(F32)
            spread_three(g4s, 32, ((p + 1) * 6 + h + 1) * 128, x, None)
    await_bytes(g4halo, recv.at[3])
    for e, p, keep in ((0, 0, sx > 0), (1, 3, sx < 31)):
        for h in range(4):
            x = g4halo[e, :, h * 128 : (h + 1) * 128].astype(F32)
            spread_three(g4s, 32, (p * 6 + h + 1) * 128, x, keep)
    for p in range(2):
        back = mm(wb4[:, :864], taps_of(g4s, p)).astype(BF)
        for h in range(4):
            rs_send[p * 4 + h] = back[:, h * 128 : (h + 1) * 128]

    def send_back(k):
        other = lax.rem(cell + k, 8)
        push(rs_send.at[other], rs_recv.at[cell], 4, (sx, lax.rem(other, 4), lax.div(other, 4)))
    loop(8, send_back)

    def scatter(count, where, shards, src, dst, mine, slot):
        def step(k):
            other, place = where(k)

            @pl.when(other < shards)
            def _():
                push(src.at[other], dst.at[mine], slot, place)
        loop(count, step)

    def spread(count, where, src, dst, slot):
        loop(count, lambda k: push(src, dst, slot, where(k)[1]))

    def total(ref):
        return jnp.sum(ref[...].astype(F32), axis=0)

    scatter(32, depth, N4, a4, in4, sx, 8)
    rs_recv[cell] = rs_send[cell]
    await_bytes(rs_recv.at[pl.ds(0, 7)], recv.at[4])
    grad_three = (total(rs_recv) * smooth_slope(p3[cell])).astype(BF)
    g3own[...] = grad_three
    g3buf[5] = grad_three

    def send_three(k):
        slot = lax.rem(5 + k, 16)
        up = lax.div(slot, 4) - 1
        side = lax.rem(slot, 4) - 1
        push(g3own, g3buf.at[slot], 5, block_place(g - up, sy - side))
    loop(16, send_three)

    for kd in range(3):
        for kh in range(3):
            at = pl.multiple_of(((ch + 1 + kd) * 6 + sy + kh) * 128, 128)
            part = mm_nt(x2s[:, pl.ds(at, 128)], grad_three).astype(BF)
            for kw in range(3):
                a3[9 * kd + 3 * kh + kw] = part[kw * 64 : (kw + 1) * 64]
    scatter(32, plane, N3, a3, in3, rank, 9)

    @pl.when(sx < N4)
    def _():
        in4[sx] = a4[sx]
        await_bytes(in4.at[pl.ds(0, 31)], recv.at[8])
        all4[sx] = total(in4).astype(BF)
        spread(32, depth, all4.at[sx], all4.at[sx], 10)

    await_bytes(g3buf.at[pl.ds(0, 15)], recv.at[5])
    for d in range(4):
        for h in range(4):
            keep = (g - 1 + d >= 0) & (g - 1 + d < 64) & (sy - 1 + h >= 0) & (sy - 1 + h < 4)
            spread_three(g3s, 128, (d * 4 + h) * 128, g3buf[d * 4 + h].astype(F32), keep)
    await_bytes(s2buf.at[pl.ds(0, 3)], recv.at[2])
    for a in range(2):
        around = jnp.concatenate(
            [g3s[:, ((a + kd) * 4 + kh) * 128 : ((a + kd) * 4 + kh + 2) * 128] for kd in range(3) for kh in range(3)],
            axis=0,
        )
        back = mm(w3b[...], around)
        for b in range(2):
            x = back[:, b * 128 : (b + 1) * 128] * s2buf[a * 2 + b]
            if a or b:
                keep = (g + a < 64) & (sy + b < 4)
                x = jnp.where(keep, x, 0.0)
            x = x.astype(BF)
            r = (a * 2 + b) * 128
            g2st[r : r + 64, :] = x
            g2st[r + 64 : r + 128, :] = from_right(x.astype(F32)).astype(BF)
    back_one = mm(wbk[...], g2st[...])
    slope_one = smooth_slope(p1[...])
    grad_one = jnp.concatenate(
        [back_one[k * 64 : (k + 1) * 64] * slope_one[:, k * 128 : (k + 1) * 128] for k in range(4)], axis=1
    ).astype(BF)
    banded = mm_nt(grad_one, vst[:, 256:])
    high = banded.astype(BF)
    rest = (banded - high.astype(F32)).astype(BF)
    local_one = jnp.zeros((32, 128), F32)
    for b in range(2):
        local_one += mm_nt(high[b * 32 : (b + 1) * 32], band[b + 1])
        local_one += mm_nt(rest[b * 32 : (b + 1) * 32], band[b + 1])
    local_one = local_one.astype(BF)
    a2[28] = local_one[:16]
    a2[29] = local_one[16:]
    grad_two = g2st[0:64, :]
    for k in range(7):
        size = 128 if k < 6 else 96
        part = mm_nt(grad_two, a1[k * 128 : k * 128 + size, :]).astype(BF)
        if k == 6:
            part = jnp.concatenate([part, jnp.zeros((64, 32), BF)], axis=1)
        for r in range(4):
            a2[k * 4 + r] = part[r * 16 : (r + 1) * 16]
    scatter(32, plane, N2, a2, in2, rank, 11)

    @pl.when(rank < N3)
    def _():
        in3[rank] = a3[rank]
        await_bytes(in3.at[pl.ds(0, 31)], recv.at[9])
        part3[...] = total(in3).astype(BF)
        mid3[z] = part3[...]
        spread(8, column, part3, mid3.at[z], 12)

    @pl.when(rank < N2)
    def _():
        in2[rank] = a2[rank]
        await_bytes(in2.at[pl.ds(0, 31)], recv.at[11])
        part2[...] = total(in2).astype(BF)
        mid2[z] = part2[...]
        spread(8, column, part2, mid2.at[z], 13)

    @pl.when(rank < N3)
    def _():
        await_bytes(mid3.at[pl.ds(0, 7)], recv.at[12])
        all3[rank] = total(mid3).astype(BF)
        spread(32, plane, all3.at[rank], all3.at[rank], 14)

    @pl.when(rank < N2)
    def _():
        await_bytes(mid2.at[pl.ds(0, 7)], recv.at[13])
        all2[rank] = total(mid2).astype(BF)
        spread(32, plane, all2.at[rank], all2.at[rank], 15)

    def arrived(me, shards, buf, slot):
        @pl.when(me < shards)
        def _():
            await_bytes(buf.at[pl.ds(0, shards - 1)], recv.at[slot])

        @pl.when(me >= shards)
        def _():
            await_bytes(buf.at[pl.ds(0, shards)], recv.at[slot])

    arrived(sx, N4, all4, 10)
    for t in range(27):
        o4[:, t * 128 : (t + 1) * 128] = all4[t].astype(F32)
    arrived(rank, N3, all3, 14)
    for k in range(14):
        if k < 13:
            pair = jnp.concatenate([all3[2 * k], all3[2 * k + 1]], axis=0)
            o3[:, k * 128 : (k + 1) * 128] = pair.astype(F32).T
        else:
            o3[:, 1664:1728] = all3[26].astype(F32).T
    arrived(rank, N2, all2, 15)
    for k in range(7):
        size = 128 if k < 6 else 96
        for r in range(4):
            o2[r * 16 : (r + 1) * 16, k * 128 : k * 128 + size] = all2[k * 4 + r].astype(F32)[:, :size]
    o1[0:16, :] = all2[28].astype(F32)[:, :108]
    o1[16:32, :] = all2[29].astype(F32)[:, :108]

    await_bytes(vin, send.at[0])
    await_bytes(gath.at[pl.ds(0, 23)], send.at[1])
    await_bytes(s2buf.at[pl.ds(0, 3)], send.at[2])
    await_bytes(g4send, send.at[3])
    await_bytes(rs_send.at[pl.ds(0, 7)], send.at[4])
    await_bytes(g3buf.at[pl.ds(0, 15)], send.at[5])

    def sent(me, shards, src, slot):
        @pl.when(me < shards)
        def _():
            await_bytes(src.at[pl.ds(0, shards - 1)], send.at[slot])

        @pl.when(me >= shards)
        def _():
            await_bytes(src.at[pl.ds(0, shards)], send.at[slot])

    sent(sx, N4, a4, 8)
    sent(rank, N3, a3, 9)
    sent(rank, N2, a2, 11)

    @pl.when(sx < N4)
    def _():
        await_bytes(in4.at[pl.ds(0, 31)], send.at[10])

    @pl.when(rank < N3)
    def _():
        await_bytes(mid3.at[pl.ds(0, 7)], send.at[12])
        await_bytes(in3.at[pl.ds(0, 31)], send.at[14])

    @pl.when(rank < N2)
    def _():
        await_bytes(mid2.at[pl.ds(0, 7)], send.at[13])
        await_bytes(in2.at[pl.ds(0, 31)], send.at[15])


def per_device(volume, w_first, w_second, w_third, w_deep, grad_out):
    cells = 2 * lax.axis_size("sx") * 4 * 128
    scale = 1.0 / float(cells) ** 0.5
    vmem = pl.BlockSpec(memory_space=pltpu.VMEM)

    def kernel(*refs):
        whole_kernel(*refs, scale)

    outs = pl.pallas_call(
        kernel,
        out_shape=(
            jax.ShapeDtypeStruct((32, 1024), BF),
            jax.ShapeDtypeStruct((32, 108), F32),
            jax.ShapeDtypeStruct((64, 864), F32),
            jax.ShapeDtypeStruct((128, 1728), F32),
            jax.ShapeDtypeStruct((32, 3456), F32),
        ),
        in_specs=[vmem] * 8,
        out_specs=(vmem,) * 5,
        scratch_shapes=[
            pltpu.VMEM((512, 512), BF),
            pltpu.VMEM((96, 288), BF),
            pltpu.VMEM((512, 256), BF),
            pltpu.VMEM((256, 512), BF),
            pltpu.VMEM((896, 128), BF),
            pltpu.VMEM((128, 896), BF),
            pltpu.VMEM((64, 3456), BF),
            pltpu.VMEM((3, 64, 512), BF),
            pltpu.VMEM((288, 768), BF),
            pltpu.VMEM((64, 512), F32),
            pltpu.VMEM((864, 128), BF),
            pltpu.VMEM((24, 64, 128), BF),
            pltpu.VMEM((192, 36 * 128), BF),
            pltpu.VMEM((64, 128), F32),
            pltpu.VMEM((4, 64, 128), F32),
            pltpu.VMEM((8, 128, 128), F32),
            pltpu.VMEM((384, 24 * 128), BF),
            pltpu.VMEM((2, 32, 512), BF),
            pltpu.VMEM((2, 32, 512), BF),
            pltpu.VMEM((96, 24 * 128), BF),
            pltpu.VMEM((8, 128, 128), BF),
            pltpu.VMEM((8, 128, 128), BF),
            pltpu.VMEM((128, 128), BF),
            pltpu.VMEM((16, 128, 128), BF),
            pltpu.VMEM((384, 16 * 128), BF),
            pltpu.VMEM((512, 128), BF),
            pltpu.VMEM((N3, 64, 128), BF),
            pltpu.VMEM((N2, 16, 128), BF),
            pltpu.VMEM((N4, 32, 128), BF),
            pltpu.VMEM((32, 64, 128), BF),
            pltpu.VMEM((32, 16, 128), BF),
            pltpu.VMEM((32, 32, 128), BF),
            pltpu.VMEM((8, 64, 128), BF),
            pltpu.VMEM((8, 16, 128), BF),
            pltpu.VMEM((64, 128), BF),
            pltpu.VMEM((16, 128), BF),
            pltpu.VMEM((N3, 64, 128), BF),
            pltpu.VMEM((N2, 16, 128), BF),
            pltpu.VMEM((N4, 32, 128), BF),
            pltpu.SemaphoreType.DMA((16,)),
            pltpu.SemaphoreType.DMA((16,)),
        ],
        compiler_params=pltpu.CompilerParams(
            collective_id=1, has_side_effects=True, vmem_limit_bytes=48 * 1024 * 1024
        ),
        name="forward_and_backward",
    )(
        volume.reshape(64, 512),
        w_first,
        w_second,
        w_third,
        w_deep,
        grad_out.reshape(32, 1024),
        jnp.asarray(row_choice(), BF),
        jnp.asarray(band_choice(), BF),
    )
    activ, grad_w1, grad_w2, grad_w3, grad_w4 = outs
    return (activ.reshape(32, 2, 4, 128), grad_w1, grad_w2, grad_w3, grad_w4)


def solution(mesh):
    placed = (
        P(None, ("sx", "ch"), "sy", None),
        P(),
        P(),
        P(),
        P(("sy", "ch"), None),
        P(("sy", "ch"), "sx", None, None),
    )
    return jax.shard_map(
        per_device,
        mesh=mesh,
        in_specs=placed,
        out_specs=(P(("sy", "ch"), "sx", None, None), P(), P(), P(), P(("sy", "ch"), None)),
        check_vma=False,
    )
```

time: 721 us -> 82.5 us (0.11)
  waiting for transfers between devices: 403 us -> 0 us
  blocking collectives: 105 us -> 0 us
  local copies, waits for them, and re-layouts: 95.9 us -> 6.17 us
  Pallas kernels: 0 us -> 75.4 us
  starting transfers between devices: 66.9 us -> 0 us
  matrix products: 21.7 us -> 0 us
  between operations: 16.9 us -> 0.75 us
  other arithmetic: 9.2 us -> 0 us
    psum x2 -> x0, waiting for transfers between devices: 374 us -> none  [the longest x1 201 us: per_device(): grad_w4 = lax.psum(local_w4.astype(jnp.bfloat16), 'sx').astype(jnp.float32)]
    psum x1 -> x0, blocking collectives: 78.5 us -> none  [per_device(): lax.psum((local_w1, local_w2, local_w3), ('sx', 'sy', 'ch'))]
    pallas_call x0 -> x1, Pallas kernels: none -> 75.4 us  [per_device(): pl.pallas_call(kernel, out_shape=(jax.ShapeDtypeStruct((32, 1024), BF), j...]
    ppermute x18 -> x0, starting transfers between devices: 66.5 us -> none  [the longest x6 27.8 us: padded_2(): before = lax.ppermute(last, axis, up)]
    slice x67 -> x0, local copies, waits for them, and re-layouts: 46.2 us -> none  [the longest x62 45.4 us: tap_block(): padded[:, depth_tap:depth_tap + stride * (depth - 1) + 1:stride, row_tap:...]
    ppermute x18 -> x0, waiting for transfers between devices: 29.2 us -> none  [the longest x6 18 us: padded_2(): after = lax.ppermute(first, axis, down)]
    all_gather x1 -> x0, blocking collectives: 26.5 us -> none  [per_device(): gathered = lax.all_gather(act_three[None], ('sy', 'ch'), axis=0, tiled=True)]
    unnamed x144 -> x17, local copies, waits for them, and re-layouts: 28.1 us -> 4.58 us
  transfers between devices with their start and end apart: 21 -> 0, of which waited for: 14 -> 0; matrix products, arithmetic and copies ran while one was open for 3% -> 0% of each run, Pallas kernels for 0% -> 0%
where the time goes in v2:
time: 82.5 us; the launch traced here: 82.3 us
  Pallas kernels  75.4 us (91%)
  local copies, waits for them, and re-layouts  6.17 us (7%)
    pallas_call x1, Pallas kernels, per_device(): pl.pallas_call(kernel, out_shape=(jax.ShapeDtypeStruct((32, 1024), BF), j...  75.4 us
    unnamed x17, local copies, waits for them, and re-layouts  4.58 us

profile of v2, /device:TPU:1, one launch (start us, length us, event | category | flops | bytes accessed | tf_op | source)
XLA Modules:
  0.0 82.3 jit_solution(6324125687874204232)
XLA Ops:
  0.6 0.0 copy-start.5
  0.6 0.9 %reshape.19.refs_0_ = bf16[64,512]{1,0:T(8,128)(2,1)S(1)} reshape(bf16[4,4,4,512]{3,2,1,0:T(4,128)(2,1)} %param.8) | data formatting | bytes 131072 | tf_op jit(solution)/shard_map/reshape | solution.py:546
  1.5 0.0 copy-done.5
  1.6 0.0 copy-start
  1.6 0.0 copy-start.1
  1.6 0.0 copy-start.2
  1.6 0.0 copy-start.3
  1.6 0.0 copy-start.4
  1.6 1.3 %copy.13.refs_3_ = bf16[128,1728]{1,0:T(8,128)(2,1)S(1)} copy(bf16[128,1728]{0,1:T(8,128)(2,1)} %param.11) | data formatting | bytes 884736 | tf_op args[3]
  2.9 0.0 copy-done
  2.9 0.0 copy-done.1
  2.9 0.0 copy-done.2
  3.0 0.0 copy-done.3
  3.0 0.0 copy-done.4
  3.0 75.4 %forward_and_backward.1 = (bf16[32,1024]{1,0:T(8,128)(2,1)S(1)}, f32[32,108]{1,0:T(8,128)S(1)}, f32[64,864]{1,0:T(8,128)S(1)}, f32[128,1728]{1,0:T(8,128)S(1)}, f32[32,3456]{1,0:T(8,128)S(1)}) custom-call(bf16[64,512]{1,0:T(8,128)(2,1)S(1)} %reshape.19.refs_0_, bf16[32,108]{1,0:T(8,128)(2,1)S(1)} %copy-done.4, bf16[64,864]{1,0:T(8,128)(2,1)S(1)} %copy-done.2, ...), custom_call_target="tpu_custom_call" | custom-call | tf_op jit(solution)/shard_map/forward_and_backward/pallas_call | solution.py:487
  78.4 0.7 reshape.21
  79.1 1.2 %copy.14 = f32[128,1728]{0,1:T(8,128)} copy(f32[128,1728]{1,0:T(8,128)S(1)} %get-tuple-element.18) | data formatting | bytes 1769472
  80.3 0.6 copy.18
  80.9 0.7 copy.19
  81.6 0.8 copy.20
  (1 shorter events, 0.0 us)
Async XLA Ops:
  0.6 0.9 %copy-start.5 = (bf16[32,2,4,128]{3,2,1,0:T(4,128)(2,1)S(1)}, bf16[32,2,4,128]{3,2,1,0:T(4,128)(2,1)}, u32[]{:S(2)}) copy-start(bf16[32,2,4,128]{3,2,1,0:T(4,128)(2,1)} %param.13) | copy-start | bytes 196612
  1.6 1.3 %copy-start = (bf16[3,128,288]{2,1,0:T(8,128)(2,1)S(1)}, bf16[3,128,288]{2,1,0:T(8,128)(2,1)}, u32[]{:S(2)}) copy-start(bf16[3,128,288]{2,1,0:T(8,128)(2,1)} %constant.5.clone.refs_7_) | copy-start | bytes 663556
  1.6 1.3 %copy-start.1 = (bf16[32,3456]{1,0:T(8,128)(2,1)S(1)}, bf16[32,3456]{1,0:T(8,128)(2,1)}, u32[]{:S(2)}) copy-start(bf16[32,3456]{1,0:T(8,128)(2,1)} %refs_4_.1) | copy-start | bytes 663556
  1.6 1.3 %copy-start.2 = (bf16[64,864]{1,0:T(8,128)(2,1)S(1)}, bf16[64,864]{1,0:T(8,128)(2,1)}, u32[]{:S(2)}) copy-start(bf16[64,864]{1,0:T(8,128)(2,1)} %refs_2_.1) | copy-start | bytes 331780
  1.6 1.3 %copy-start.3 = (bf16[224,256]{1,0:T(8,128)(2,1)S(1)}, bf16[224,256]{1,0:T(8,128)(2,1)}, u32[]{:S(2)}) copy-start(bf16[224,256]{1,0:T(8,128)(2,1)} %constant.4.clone.refs_6_) | copy-start | bytes 344068
  1.6 1.3 %copy-start.4 = (bf16[32,108]{1,0:T(8,128)(2,1)S(1)}, bf16[32,108]{1,0:T(8,128)(2,1)}, u32[]{:S(2)}) copy-start(bf16[32,108]{1,0:T(8,128)(2,1)} %refs_1_.1) | copy-start | bytes 20740

commit v3 on v2

--- a/solution.py
+++ b/solution.py
@@ -9,7 +9,7 @@
 MESH = pl.DeviceIdType.MESH
 BF = jnp.bfloat16
 F32 = jnp.float32
-N3, N2, N4 = 27, 30, 27
+HALF = 14
 
 
 def row_choice():
@@ -68,12 +68,12 @@
 
 
 def whole_kernel(
-    vol, w1, w2, w3, w4, gout, rows_pick, band,
-    activ, o1, o2, o3, o4,
-    perm, w1band, wbk_t, wbk, wb4_t, wb4, w3b,
+    vol, w1, w2, w3t, w4, gout, rows_pick, band,
+    activ, out2, out3, out4,
+    perm, w1band, wbk_t, wbk, wb4_t, wb4, w3, w3b,
     vin, vst, p1, a1, gath, x2s, s2own, s2buf, p3, x3s,
     g4send, g4halo, g4s, rs_send, rs_recv, g3own, g3buf, g3s, g2st,
-    a3, a2, a4, in3, in2, in4, mid3, mid2, part3, part2, all3, all2, all4,
+    a3, a2, a4, pair3, pair4, sum3, sum4, in3, in2, in4, mid3, mid2, part3, part2, all3, all2, all4,
     send, recv, scale,
 ):
     sx, sy, ch = lax.axis_index("sx"), lax.axis_index("sy"), lax.axis_index("ch")
@@ -81,6 +81,8 @@
     z = lax.rem(lax.div(sx, 2), 8)
     low = lax.div(sx, 16)
     rank = low * 16 + core * 8 + ch * 4 + sy
+    rank3 = low * 8 + ch * 4 + sy
+    rank4 = low * 8 + z
     g = sx * 2 + ch
     cell = ch * 4 + sy
 
@@ -88,33 +90,58 @@
         d = lax.rem(depth_block + 64, 64)
         return (lax.div(d, 2), lax.rem(row_block + 4, 4), lax.rem(d, 2))
 
-    def near(k):
-        other = lax.rem(cell + 8 + k, 24)
-        group = lax.div(other, 8) - 1
-        return group, (lax.rem(sx + group + 32, 32), lax.rem(other, 4), lax.rem(lax.div(other, 4), 2))
-
-    def plane(k):
-        other = lax.rem(rank + k, 32)
-        place = (
-            lax.div(other, 16) * 16 + z * 2 + lax.rem(lax.div(other, 8), 2),
-            lax.rem(other, 4),
-            lax.rem(lax.div(other, 4), 2),
-        )
-        return other, place
-
-    def column(k):
-        other = lax.rem(z + k, 8)
-        return other, (low * 16 + other * 2 + core, sy, ch)
-
-    def depth(k):
-        other = lax.rem(sx + k, 32)
-        return other, (other, sy, ch)
-
-    def loop(count, step, start=1):
-        def body(k, carry):
-            step(k)
-            return carry
-        lax.fori_loop(start, count, body, 0)
+    def wrap(value, size):
+        return jnp.where(value >= size, value - size, value)
+
+    xs = [sy] + [wrap(sy + k, 4) for k in (1, 2, 3)]
+    chs = (ch, 1 - ch)
+    cores = (core, 1 - core)
+    lows = (low, 1 - low)
+    groups = {-1: wrap(sx + 31, 32), 0: sx, 1: wrap(sx + 1, 32)}
+    ring = (0, 1, 2, 1)
+
+    near = []
+    for far in range(4, -1, -1):
+        for dg in (-1, 1, 0):
+            for dx in range(4):
+                for dc in range(2):
+                    if ring[dx] + 2 * dc == far and (dg or dx or dc):
+                        near.append((dg, (groups[dg], xs[dx], chs[dc])))
+    plane = []
+    mates = []
+    for far in range(5, -1, -1):
+        for dl in range(2):
+            for dn in range(2):
+                group = lows[dl] * 16 + z * 2 + cores[dn]
+                first = lows[dl] * 16 + cores[dn] * 8
+                for dx in range(4):
+                    for dc in range(2):
+                        if ring[dx] + 2 * dc + dl == far and (dl or dn or dx or dc):
+                            entry = (first + chs[dc] * 4 + xs[dx], (group, xs[dx], chs[dc]))
+                            plane.append(entry)
+                            if dl or dn:
+                                mates.append(entry)
+    column = []
+    for k in (4, 3, 5, 2, 6, 1, 7):
+        other = wrap(z + k, 8)
+        column.append((other, (low * 16 + other * 2 + core, sy, ch)))
+    mate = (sx + 1 - 2 * core, sy, ch)
+    square = []
+    for far in range(5, -1, -1):
+        for dl in range(2):
+            for dx in range(4):
+                for dc in range(2):
+                    if ring[dx] + 2 * dc + dl == far and (dl or dx or dc):
+                        other = lows[dl] * 8 + chs[dc] * 4 + xs[dx]
+                        square.append((other, (lows[dl] * 16 + z * 2 + core, xs[dx], chs[dc])))
+    line = []
+    for k in (4, 3, 5, 2, 6, 1, 7, 0):
+        for dl in (1, 0):
+            if k or dl:
+                there = wrap(z + k, 8)
+                line.append((lows[dl] * 8 + there, (lows[dl] * 16 + there * 2 + core, sy, ch), k))
+    beyond = [(other, place) for other, place, k in line if k]
+    line = [(other, place) for other, place, k in line]
 
     def push(src, dst, slot, place):
         pltpu.make_async_remote_copy(
@@ -124,27 +151,14 @@
 
     barrier = pltpu.get_barrier_semaphore()
 
-    def greet(count, where):
-        def step(k):
-            pl.semaphore_signal(barrier, inc=1, device_id=where(k)[1], device_id_type=MESH)
-        loop(count, step)
-
-    greet(24, near)
-    greet(32, plane)
-    greet(8, column)
-    greet(32, depth)
+    for other, place in near + mates + beyond:
+        pl.semaphore_signal(barrier, inc=1, device_id=place, device_id_type=MESH)
 
     for p in range(4):
         r = lax.broadcasted_iota(jnp.int32, (512, 128), 0)
         perm[:, p * 128 : (p + 1) * 128] = jnp.where(r == 4 * lane_of((512, 128)) + p, 1.0, 0.0).astype(BF)
     for j in range(3):
         w1band[j * 32 : (j + 1) * 32, :] = mm(w1[...], band[j, :108, :]).astype(BF)
-    pl.semaphore_wait(barrier, 23 + 31 + 7 + 31)
-
-    push(vol, vin.at[0], 0, block_place(g + 1, sy))
-    push(vol, vin.at[1], 0, block_place(g, sy + 1))
-    push(vol, vin.at[2], 0, block_place(g + 1, sy + 1))
-
     zero = jnp.zeros((96, 128), BF)
     for d in range(6):
         for h in (0, 5):
@@ -158,16 +172,18 @@
     for t in range(27):
         wb4_t[t * 32 : (t + 1) * 32, :] = w4[:, (26 - t) * 128 : (27 - t) * 128]
     wb4_t[864:896, :] = jnp.zeros((32, 128), BF)
+    a2[30] = jnp.zeros((16, 128), BF)
+    a3[1, 13] = jnp.zeros((64, 128), BF)
+    a4[1, 13] = jnp.zeros((32, 128), BF)
+    a2[31] = jnp.zeros((16, 128), BF)
     for k in range(7):
         wb4[:, k * 128 : (k + 1) * 128] = wb4_t[k * 128 : (k + 1) * 128, :].astype(F32).T.astype(BF)
     for k in range(14):
-        if k < 13:
-            turned = w3[:, k * 128 : (k + 1) * 128].astype(F32).T.astype(BF)
-        else:
-            turned = w3[:, 1664:1728].astype(F32).T.astype(BF)
-        w3b[:, (26 - 2 * k) * 128 : (27 - 2 * k) * 128] = turned[:64]
-        if k < 13:
-            w3b[:, (25 - 2 * k) * 128 : (26 - 2 * k) * 128] = turned[64:]
+        size = 128 if k < 13 else 64
+        turned = w3t[k * 128 : k * 128 + size, :]
+        w3[:, k * 128 : k * 128 + size] = turned.astype(F32).T.astype(BF)
+    for t in range(27):
+        w3b[:, (26 - t) * 128 : (27 - t) * 128] = w3t[t * 64 : (t + 1) * 64, :]
     wbk_t[...] = jnp.zeros((512, 256), BF)
     taps = {(0, 0): 1, (1, 0): 2, (1, 1): 0}
     for (pa, a), kd in taps.items():
@@ -181,6 +197,12 @@
         for c in range(2):
             block = wbk_t[r * 128 : (r + 1) * 128, c * 128 : (c + 1) * 128]
             wbk[c * 128 : (c + 1) * 128, r * 128 : (r + 1) * 128] = block.astype(F32).T.astype(BF)
+
+    pl.semaphore_wait(barrier, 23 + 24 + 14)
+
+    push(vol, vin.at[0], 0, block_place(g + 1, sy))
+    push(vol, vin.at[1], 0, block_place(g, sy + 1))
+    push(vol, vin.at[2], 0, block_place(g + 1, sy + 1))
 
     await_bytes(vin, recv.at[0])
     none = jnp.zeros((64, 512), BF)
@@ -218,10 +240,8 @@
     own = (ch + 2) * 4 + sy
     gath[own] = act_two
 
-    def send_act(k):
-        group, place = near(k)
+    for group, place in near:
         push(gath.at[own], gath.at[own - 8 * group], 1, place)
-    loop(24, send_act)
     slope_two = smooth_slope(pre_two)
     s2own[...] = slope_two
     s2buf[0] = slope_two
@@ -276,7 +296,8 @@
                 more = mm_nt(grads[p], x3s[:, at : at + 512])
                 part = more if part is None else part + more
             for kw in range(3):
-                a4[9 * kd + 3 * kh + kw] = part[:, kw * 128 : (kw + 1) * 128].astype(BF)
+                a4[(9 * kd + 3 * kh + kw) // HALF, (9 * kd + 3 * kh + kw) % HALF] = part[:, kw * 128 : (kw + 1) * 128].astype(BF)
+    push(a4.at[1 - core], pair4, 16, mate)
     for p in range(2):
         for h in range(4):
             x = grads[p][:, h * 128 : (h + 1) * 128].astype(F32)
@@ -291,54 +312,60 @@
         for h in range(4):
             rs_send[p * 4 + h] = back[:, h * 128 : (h + 1) * 128]
 
-    def send_back(k):
-        other = lax.rem(cell + k, 8)
-        push(rs_send.at[other], rs_recv.at[cell], 4, (sx, lax.rem(other, 4), lax.div(other, 4)))
-    loop(8, send_back)
-
-    def scatter(count, where, shards, src, dst, mine, slot):
-        def step(k):
-            other, place = where(k)
-
-            @pl.when(other < shards)
-            def _():
+    for group, place in near:
+        if place[0] is sx:
+            push(rs_send.at[place[2] * 4 + place[1]], rs_recv.at[cell], 4, place)
+
+    def scatter(places, shards, src, dst, mine, slot):
+        for other, place in places:
+            if shards == 32:
                 push(src.at[other], dst.at[mine], slot, place)
-        loop(count, step)
-
-    def spread(count, where, src, dst, slot):
-        loop(count, lambda k: push(src, dst, slot, where(k)[1]))
+            else:
+                @pl.when(other < shards)
+                def _():
+                    push(src.at[other], dst.at[mine], slot, place)
+
+    def spread(places, src, dst, slot):
+        for other, place in places:
+            push(src, dst, slot, place)
 
     def total(ref):
         return jnp.sum(ref[...].astype(F32), axis=0)
 
-    scatter(32, depth, N4, a4, in4, sx, 8)
+    await_bytes(pair4, recv.at[16])
+    sum4[...] = (a4[core].astype(F32) + pair4[...].astype(F32)).astype(BF)
+    scatter(line, HALF, sum4, in4, rank4, 8)
     rs_recv[cell] = rs_send[cell]
     await_bytes(rs_recv.at[pl.ds(0, 7)], recv.at[4])
     grad_three = (total(rs_recv) * smooth_slope(p3[cell])).astype(BF)
     g3own[...] = grad_three
     g3buf[5] = grad_three
 
-    def send_three(k):
-        slot = lax.rem(5 + k, 16)
-        up = lax.div(slot, 4) - 1
-        side = lax.rem(slot, 4) - 1
-        push(g3own, g3buf.at[slot], 5, block_place(g - up, sy - side))
-    loop(16, send_three)
+    for up in (-1, 1, 2, 0):
+        d = lax.rem(g - up + 64, 64)
+        group, side_ch = lax.div(d, 2), lax.rem(d, 2)
+        for side in (2, -1, 1, 0):
+            if up or side:
+                push(g3own, g3buf.at[(up + 1) * 4 + side + 1], 5, (group, xs[(-side) % 4], side_ch))
 
     for kd in range(3):
         for kh in range(3):
             at = pl.multiple_of(((ch + 1 + kd) * 6 + sy + kh) * 128, 128)
             part = mm_nt(x2s[:, pl.ds(at, 128)], grad_three).astype(BF)
             for kw in range(3):
-                a3[9 * kd + 3 * kh + kw] = part[kw * 64 : (kw + 1) * 64]
-    scatter(32, plane, N3, a3, in3, rank, 9)
-
-    @pl.when(sx < N4)
+                a3[(9 * kd + 3 * kh + kw) // HALF, (9 * kd + 3 * kh + kw) % HALF] = part[kw * 64 : (kw + 1) * 64]
+    push(a3.at[1 - core], pair3, 6, mate)
+
+    @pl.when(rank4 < HALF)
     def _():
-        in4[sx] = a4[sx]
-        await_bytes(in4.at[pl.ds(0, 31)], recv.at[8])
-        all4[sx] = total(in4).astype(BF)
-        spread(32, depth, all4.at[sx], all4.at[sx], 10)
+        in4[rank4] = sum4[rank4]
+        await_bytes(in4.at[pl.ds(0, 15)], recv.at[8])
+        all4[core, rank4] = total(in4).astype(BF)
+        spread(line, all4.at[core, rank4], all4.at[core, rank4], 10)
+
+    await_bytes(pair3, recv.at[6])
+    sum3[...] = (a3[core].astype(F32) + pair3[...].astype(F32)).astype(BF)
+    scatter(square, HALF, sum3, in3, rank3, 9)
 
     await_bytes(g3buf.at[pl.ds(0, 15)], recv.at[5])
     for d in range(4):
@@ -361,6 +388,14 @@
             r = (a * 2 + b) * 128
             g2st[r : r + 64, :] = x
             g2st[r + 64 : r + 128, :] = from_right(x.astype(F32)).astype(BF)
+    @pl.when(rank3 < HALF)
+    def _():
+        in3[rank3] = sum3[rank3]
+        await_bytes(in3.at[pl.ds(0, 15)], recv.at[9])
+        part3[...] = total(in3).astype(BF)
+        mid3[z] = part3[...]
+        spread(column, part3, mid3.at[z], 12)
+
     back_one = mm(wbk[...], g2st[...])
     slope_one = smooth_slope(p1[...])
     grad_one = jnp.concatenate(
@@ -384,56 +419,86 @@
             part = jnp.concatenate([part, jnp.zeros((64, 32), BF)], axis=1)
         for r in range(4):
             a2[k * 4 + r] = part[r * 16 : (r + 1) * 16]
-    scatter(32, plane, N2, a2, in2, rank, 11)
-
-    @pl.when(rank < N3)
-    def _():
-        in3[rank] = a3[rank]
-        await_bytes(in3.at[pl.ds(0, 31)], recv.at[9])
-        part3[...] = total(in3).astype(BF)
-        mid3[z] = part3[...]
-        spread(8, column, part3, mid3.at[z], 12)
-
-    @pl.when(rank < N2)
-    def _():
-        in2[rank] = a2[rank]
-        await_bytes(in2.at[pl.ds(0, 31)], recv.at[11])
-        part2[...] = total(in2).astype(BF)
-        mid2[z] = part2[...]
-        spread(8, column, part2, mid2.at[z], 13)
-
-    @pl.when(rank < N3)
+    scatter(plane, 32, a2, in2, rank, 11)
+
+    @pl.when(rank3 < HALF)
     def _():
         await_bytes(mid3.at[pl.ds(0, 7)], recv.at[12])
-        all3[rank] = total(mid3).astype(BF)
-        spread(32, plane, all3.at[rank], all3.at[rank], 14)
-
-    @pl.when(rank < N2)
+        all3[core, rank3] = total(mid3).astype(BF)
+        spread(square, all3.at[core, rank3], all3.at[core, rank3], 14)
+
+    in2[rank] = a2[rank]
+    await_bytes(in2.at[pl.ds(0, 31)], recv.at[11])
+    part2[...] = total(in2).astype(BF)
+    mid2[z] = part2[...]
+    spread(column, part2, mid2.at[z], 13)
+
+    await_bytes(mid2.at[pl.ds(0, 7)], recv.at[13])
+    all2[rank] = total(mid2).astype(BF)
+    spread(plane, all2.at[rank], all2.at[rank], 15)
+
+    def arrived(me, buf, slot):
+        @pl.when(me < HALF)
+        def _():
+            await_bytes(buf.at[0, pl.ds(0, HALF - 1)], recv.at[slot])
+
+        @pl.when(me >= HALF)
+        def _():
+            await_bytes(buf.at[0], recv.at[slot])
+
+    arrived(rank4, all4, 10)
+    push(all4.at[core], all4.at[core], 17, mate)
+    arrived(rank3, all3, 14)
+    push(all3.at[core], all3.at[core], 7, mate)
+    await_bytes(all4.at[0], recv.at[17])
+    out4[...] = all4[...]
+    await_bytes(all3.at[0], recv.at[7])
+    out3[...] = all3[...]
+    await_bytes(all2.at[pl.ds(0, 31)], recv.at[15])
+    out2[...] = all2[...]
+
+    await_bytes(vin, send.at[0])
+    await_bytes(gath.at[pl.ds(0, 23)], send.at[1])
+    await_bytes(s2buf.at[pl.ds(0, 3)], send.at[2])
+    await_bytes(g4send, send.at[3])
+    await_bytes(rs_send.at[pl.ds(0, 7)], send.at[4])
+    await_bytes(g3buf.at[pl.ds(0, 15)], send.at[5])
+
+    await_bytes(in2.at[pl.ds(0, 31)], send.at[11])
+    for pair, total_sum, gathered, slots in ((pair4, sum4, all4, (16, 8, 10, 17)), (pair3, sum3, all3, (6, 9, 14, 7))):
+        me = rank4 if pair is pair4 else rank3
+        await_bytes(pair, send.at[slots[0]])
+        await_bytes(gathered.at[0], send.at[slots[3]])
+
+        @pl.when(me < HALF)
+        def _():
+            await_bytes(total_sum.at[pl.ds(0, HALF - 1)], send.at[slots[1]])
+
+        @pl.when(me >= HALF)
+        def _():
+            await_bytes(total_sum, send.at[slots[1]])
+
+    @pl.when(rank4 < HALF)
     def _():
-        await_bytes(mid2.at[pl.ds(0, 7)], recv.at[13])
-        all2[rank] = total(mid2).astype(BF)
-        spread(32, plane, all2.at[rank], all2.at[rank], 15)
-
-    def arrived(me, shards, buf, slot):
-        @pl.when(me < shards)
-        def _():
-            await_bytes(buf.at[pl.ds(0, shards - 1)], recv.at[slot])
-
-        @pl.when(me >= shards)
-        def _():
-            await_bytes(buf.at[pl.ds(0, shards)], recv.at[slot])
-
-    arrived(sx, N4, all4, 10)
+        await_bytes(in4.at[pl.ds(0, 15)], send.at[10])
+
+    @pl.when(rank3 < HALF)
+    def _():
+        await_bytes(mid3.at[pl.ds(0, 7)], send.at[12])
+        await_bytes(in3.at[pl.ds(0, 15)], send.at[14])
+
+    await_bytes(mid2.at[pl.ds(0, 7)], send.at[13])
+    await_bytes(in2.at[pl.ds(0, 31)], send.at[15])
+
+
+def finish_kernel(act, all2, all3, all4, activ, o1, o2, o3, o4):
+    for p in range(2):
+        for h in range(4):
+            at = (p * 4 + h) * 128
+            activ[:, p, h, :] = act[:, at : at + 128]
     for t in range(27):
-        o4[:, t * 128 : (t + 1) * 128] = all4[t].astype(F32)
-    arrived(rank, N3, all3, 14)
-    for k in range(14):
-        if k < 13:
-            pair = jnp.concatenate([all3[2 * k], all3[2 * k + 1]], axis=0)
-            o3[:, k * 128 : (k + 1) * 128] = pair.astype(F32).T
-        else:
-            o3[:, 1664:1728] = all3[26].astype(F32).T
-    arrived(rank, N2, all2, 15)
+        o4[:, t * 128 : (t + 1) * 128] = all4[t // HALF, t % HALF].astype(F32)
+        o3[t * 64 : (t + 1) * 64, :] = all3[t // HALF, t % HALF].astype(F32)
     for k in range(7):
         size = 128 if k < 6 else 96
         for r in range(4):
@@ -441,40 +506,6 @@
     o1[0:16, :] = all2[28].astype(F32)[:, :108]
     o1[16:32, :] = all2[29].astype(F32)[:, :108]
 
-    await_bytes(vin, send.at[0])
-    await_bytes(gath.at[pl.ds(0, 23)], send.at[1])
-    await_bytes(s2buf.at[pl.ds(0, 3)], send.at[2])
-    await_bytes(g4send, send.at[3])
-    await_bytes(rs_send.at[pl.ds(0, 7)], send.at[4])
-    await_bytes(g3buf.at[pl.ds(0, 15)], send.at[5])
-
-    def sent(me, shards, src, slot):
-        @pl.when(me < shards)
-        def _():
-            await_bytes(src.at[pl.ds(0, shards - 1)], send.at[slot])
-
-        @pl.when(me >= shards)
-        def _():
-            await_bytes(src.at[pl.ds(0, shards)], send.at[slot])
-
-    sent(sx, N4, a4, 8)
-    sent(rank, N3, a3, 9)
-    sent(rank, N2, a2, 11)
-
-    @pl.when(sx < N4)
-    def _():
-        await_bytes(in4.at[pl.ds(0, 31)], send.at[10])
-
-    @pl.when(rank < N3)
-    def _():
-        await_bytes(mid3.at[pl.ds(0, 7)], send.at[12])
-        await_bytes(in3.at[pl.ds(0, 31)], send.at[14])
-
-    @pl.when(rank < N2)
-    def _():
-        await_bytes(mid2.at[pl.ds(0, 7)], send.at[13])
-        await_bytes(in2.at[pl.ds(0, 31)], send.at[15])
-
 
 def per_device(volume, w_first, w_second, w_third, w_deep, grad_out):
     cells = 2 * lax.axis_size("sx") * 4 * 128
@@ -488,13 +519,12 @@
         kernel,
         out_shape=(
             jax.ShapeDtypeStruct((32, 1024), BF),
-            jax.ShapeDtypeStruct((32, 108), F32),
-            jax.ShapeDtypeStruct((64, 864), F32),
-            jax.ShapeDtypeStruct((128, 1728), F32),
-            jax.ShapeDtypeStruct((32, 3456), F32),
+            jax.ShapeDtypeStruct((32, 16, 128), BF),
+            jax.ShapeDtypeStruct((2, HALF, 64, 128), BF),
+            jax.ShapeDtypeStruct((2, HALF, 32, 128), BF),
         ),
         in_specs=[vmem] * 8,
-        out_specs=(vmem,) * 5,
+        out_specs=(vmem,) * 4,
         scratch_shapes=[
             pltpu.VMEM((512, 512), BF),
             pltpu.VMEM((96, 288), BF),
@@ -502,6 +532,7 @@
             pltpu.VMEM((256, 512), BF),
             pltpu.VMEM((896, 128), BF),
             pltpu.VMEM((128, 896), BF),
+            pltpu.VMEM((128, 1728), BF),
             pltpu.VMEM((64, 3456), BF),
             pltpu.VMEM((3, 64, 512), BF),
             pltpu.VMEM((288, 768), BF),
@@ -522,21 +553,25 @@
             pltpu.VMEM((16, 128, 128), BF),
             pltpu.VMEM((384, 16 * 128), BF),
             pltpu.VMEM((512, 128), BF),
-            pltpu.VMEM((N3, 64, 128), BF),
-            pltpu.VMEM((N2, 16, 128), BF),
-            pltpu.VMEM((N4, 32, 128), BF),
-            pltpu.VMEM((32, 64, 128), BF),
+            pltpu.VMEM((2, HALF, 64, 128), BF),
             pltpu.VMEM((32, 16, 128), BF),
-            pltpu.VMEM((32, 32, 128), BF),
+            pltpu.VMEM((2, HALF, 32, 128), BF),
+            pltpu.VMEM((HALF, 64, 128), BF),
+            pltpu.VMEM((HALF, 32, 128), BF),
+            pltpu.VMEM((HALF, 64, 128), BF),
+            pltpu.VMEM((HALF, 32, 128), BF),
+            pltpu.VMEM((16, 64, 128), BF),
+            pltpu.VMEM((32, 16, 128), BF),
+            pltpu.VMEM((16, 32, 128), BF),
             pltpu.VMEM((8, 64, 128), BF),
             pltpu.VMEM((8, 16, 128), BF),
             pltpu.VMEM((64, 128), BF),
             pltpu.VMEM((16, 128), BF),
-            pltpu.VMEM((N3, 64, 128), BF),
-            pltpu.VMEM((N2, 16, 128), BF),
-            pltpu.VMEM((N4, 32, 128), BF),
-            pltpu.SemaphoreType.DMA((16,)),
-            pltpu.SemaphoreType.DMA((16,)),
+            pltpu.VMEM((2, HALF, 64, 128), BF),
+            pltpu.VMEM((32, 16, 128), BF),
+            pltpu.VMEM((2, HALF, 32, 128), BF),
+            pltpu.SemaphoreType.DMA((18,)),
+            pltpu.SemaphoreType.DMA((18,)),
         ],
         compiler_params=pltpu.CompilerParams(
             collective_id=1, has_side_effects=True, vmem_limit_bytes=48 * 1024 * 1024
@@ -546,14 +581,25 @@
         volume.reshape(64, 512),
         w_first,
         w_second,
-        w_third,
+        w_third.T,
         w_deep,
         grad_out.reshape(32, 1024),
         jnp.asarray(row_choice(), BF),
         jnp.asarray(band_choice(), BF),
     )
-    activ, grad_w1, grad_w2, grad_w3, grad_w4 = outs
-    return (activ.reshape(32, 2, 4, 128), grad_w1, grad_w2, grad_w3, grad_w4)
+    activ, grad_w1, grad_w2, grad_w3, grad_w4 = pl.pallas_call(
+        finish_kernel,
+        out_shape=(
+            jax.ShapeDtypeStruct((32, 2, 4, 128), BF),
+            jax.ShapeDtypeStruct((32, 108), F32),
+            jax.ShapeDtypeStruct((64, 864), F32),
+            jax.ShapeDtypeStruct((1728, 128), F32),
+            jax.ShapeDtypeStruct((32, 3456), F32),
+        ),
+        compiler_params=pltpu.CompilerParams(vmem_limit_bytes=32 * 1024 * 1024),
+        name="widen_outputs",
+    )(*outs)
+    return (activ, grad_w1, grad_w2, grad_w3.T, grad_w4)
 
 
 def solution(mesh):

time: 82.5 us -> 73.3 us (0.89)
  Pallas kernels: 75.4 us -> 66.8 us
    pallas_call x1, Pallas kernels: 75.4 us -> 65.6 us  [per_device(): pl.pallas_call(kernel, out_shape=(jax.ShapeDtypeStruct((32, 1024), BF), j...]
    pallas_call x0 -> x1, Pallas kernels: none -> 1.21 us  [per_device(): pl.pallas_call(finish_kernel, out_shape=(jax.ShapeDtypeStruct((32, 2, 4,...]
    reshape x1, local copies, waits for them, and re-layouts: 0.03 us -> 0.88 us  [per_device(): grad_out.reshape(32, 1024)]
    unnamed x17 -> x12, local copies, waits for them, and re-layouts: 4.58 us -> 3.78 us
where the time goes in v3:
time: 73.3 us; the launch traced here: 73.1 us
  Pallas kernels  66.8 us (91%)
  local copies, waits for them, and re-layouts  5.55 us (8%)
    pallas_call x1, Pallas kernels, per_device(): pl.pallas_call(kernel, out_shape=(jax.ShapeDtypeStruct((32, 1024), BF), j...  65.6 us
    unnamed x12, local copies, waits for them, and re-layouts  3.78 us

profile of v3, /device:TPU:1, one launch (start us, length us, event | category | flops | bytes accessed | tf_op | source)
XLA Modules:
  0.0 73.1 jit_solution(3161444565130406181)
XLA Ops:
  0.6 0.0 copy-start.2
  0.6 0.9 %reshape.16.refs_0_ = bf16[64,512]{1,0:T(8,128)(2,1)S(1)} reshape(bf16[4,4,4,512]{3,2,1,0:T(4,128)(2,1)} %param.8) | data formatting | bytes 131072 | tf_op jit(solution)/shard_map/reshape | solution.py:581
  1.5 0.0 copy-start.5
  1.6 0.9 %reshape.17.refs_5_ = bf16[32,1024]{1,0:T(8,128)(2,1)S(1)} reshape(bf16[32,2,4,128]{3,2,1,0:T(4,128)(2,1)} %param.13) | data formatting | bytes 131072 | tf_op jit(solution)/shard_map/reshape | solution.py:586
  2.4 0.0 copy-done.2
  2.4 0.0 copy-done.5
  2.5 0.0 copy-start
  2.5 1.0 %copy-done = bf16[128,1728]{0,1:T(8,128)(2,1)S(1)} copy-done((bf16[128,1728]{0,1:T(8,128)(2,1)S(1)}, bf16[128,1728]{0,1:T(8,128)(2,1)}, u32[]{:S(2)}) %copy-start) | copy-done | bytes 442392
  3.5 0.0 copy-start.1
  3.5 1.0 %copy-done.1 = bf16[3,128,288]{2,1,0:T(8,128)(2,1)S(1)} copy-done((bf16[3,128,288]{2,1,0:T(8,128)(2,1)S(1)}, bf16[3,128,288]{2,1,0:T(8,128)(2,1)}, u32[]{:S(2)}) %copy-start.1) | copy-done | bytes 221208
  4.4 0.0 copy-start.3
  4.4 0.9 %copy-done.3 = bf16[64,864]{1,0:T(8,128)(2,1)S(1)} copy-done((bf16[64,864]{1,0:T(8,128)(2,1)S(1)}, bf16[64,864]{1,0:T(8,128)(2,1)}, u32[]{:S(2)}) %copy-start.3) | copy-done | bytes 110616
  5.3 0.0 copy-start.4
  5.3 0.9 %copy-done.4 = bf16[224,256]{1,0:T(8,128)(2,1)S(1)} copy-done((bf16[224,256]{1,0:T(8,128)(2,1)S(1)}, bf16[224,256]{1,0:T(8,128)(2,1)}, u32[]{:S(2)}) %copy-start.4) | copy-done | bytes 114712
  6.2 65.6 %forward_and_backward.1 = (bf16[32,1024]{1,0:T(8,128)(2,1)S(1)}, bf16[32,16,128]{2,1,0:T(8,128)(2,1)S(1)}, bf16[2,14,64,128]{3,2,1,0:T(8,128)(2,1)S(1)}, bf16[2,14,32,128]{3,2,1,0:T(8,128)(2,1)S(1)}) custom-call(bf16[64,512]{1,0:T(8,128)(2,1)S(1)} %reshape.16.refs_0_, bf16[32,108]{1,0:T(8,128)(2,1)S(1)} %copy-done.5, bf16[64,864]{1,0:T(8,128)(2,1)S(1)} %copy-done.3, ...), custom_call_target="tpu_custom_call" | custom-call | tf_op jit(solution)/shard_map/forward_and_backward/pallas_call | solution.py:518
  71.9 1.2 %widen_outputs.1 = (bf16[32,2,4,128]{3,2,1,0:T(4,128)(2,1)}, f32[32,108]{1,0:T(8,128)}, f32[64,864]{1,0:T(8,128)}, f32[1728,128]{1,0:T(8,128)}, f32[32,3456]{1,0:T(8,128)}) custom-call(bf16[32,1024]{1,0:T(8,128)(2,1)S(1)} %get-tuple-element.14.act, bf16[32,16,128]{2,1,0:T(8,128)(2,1)S(1)} %get-tuple-element.15.all2, ...), custom_call_target="tpu_custom_call" | custom-call | tf_op jit(solution)/shard_map/widen_outputs/pallas_call | solution.py:590
Async XLA Ops:
  0.6 1.8 %copy-start.2 = (bf16[32,3456]{1,0:T(8,128)(2,1)S(1)}, bf16[32,3456]{1,0:T(8,128)(2,1)}, u32[]{:S(2)}) copy-start(bf16[32,3456]{1,0:T(8,128)(2,1)} %refs_4_.1) | copy-start | bytes 663556
  1.5 0.9 %copy-start.5 = (bf16[32,108]{1,0:T(8,128)(2,1)S(1)}, bf16[32,108]{1,0:T(8,128)(2,1)}, u32[]{:S(2)}) copy-start(bf16[32,108]{1,0:T(8,128)(2,1)} %refs_1_.1) | copy-start | bytes 20740
  2.5 1.0 %copy-start = (bf16[128,1728]{0,1:T(8,128)(2,1)S(1)}, bf16[128,1728]{0,1:T(8,128)(2,1)}, u32[]{:S(2)}) copy-start(bf16[128,1728]{0,1:T(8,128)(2,1)} %param.11) | copy-start | bytes 1327108
  3.5 1.0 %copy-start.1 = (bf16[3,128,288]{2,1,0:T(8,128)(2,1)S(1)}, bf16[3,128,288]{2,1,0:T(8,128)(2,1)}, u32[]{:S(2)}) copy-start(bf16[3,128,288]{2,1,0:T(8,128)(2,1)} %constant.5.clone.refs_7_) | copy-start | bytes 663556
  4.4 0.9 %copy-start.3 = (bf16[64,864]{1,0:T(8,128)(2,1)S(1)}, bf16[64,864]{1,0:T(8,128)(2,1)}, u32[]{:S(2)}) copy-start(bf16[64,864]{1,0:T(8,128)(2,1)} %refs_2_.1) | copy-start | bytes 331780
  5.3 0.9 %copy-start.4 = (bf16[224,256]{1,0:T(8,128)(2,1)S(1)}, bf16[224,256]{1,0:T(8,128)(2,1)}, u32[]{:S(2)}) copy-start(bf16[224,256]{1,0:T(8,128)(2,1)} %constant.4.clone.refs_6_) | copy-start | bytes 344068

commit v4 on v3

--- a/solution.py
+++ b/solution.py
@@ -68,13 +68,14 @@
 
 
 def whole_kernel(
-    vol, w1, w2, w3t, w4, gout, rows_pick, band,
-    activ, out2, out3, out4,
+    vol_in, w1_in, w2_in, w3t_in, w4_in, gout_in, rows_in, band_in,
+    activ_out, out2, out3, out4,
     perm, w1band, wbk_t, wbk, wb4_t, wb4, w3, w3b,
     vin, vst, p1, a1, gath, x2s, s2own, s2buf, p3, x3s,
     g4send, g4halo, g4s, rs_send, rs_recv, g3own, g3buf, g3s, g2st,
     a3, a2, a4, pair3, pair4, sum3, sum4, in3, in2, in4, mid3, mid2, part3, part2, all3, all2, all4,
-    send, recv, scale,
+    activ, vol_raw, gout_raw, vol, w1, w2, w3t, w4, gout, rows_pick, band,
+    send, recv, load, scale,
 ):
     sx, sy, ch = lax.axis_index("sx"), lax.axis_index("sy"), lax.axis_index("ch")
     core = lax.rem(sx, 2)
@@ -154,9 +155,30 @@
     for other, place in near + mates + beyond:
         pl.semaphore_signal(barrier, inc=1, device_id=place, device_id_type=MESH)
 
+    loads = [
+        pltpu.make_async_copy(src, dst, load.at[k])
+        for k, (src, dst) in enumerate(
+            (
+                (vol_in, vol_raw), (w1_in, w1), (band_in, band), (w4_in, w4), (w3t_in, w3t),
+                (w2_in, w2), (rows_in, rows_pick), (gout_in, gout_raw),
+            )
+        )
+    ]
+    for each in loads:
+        each.start()
+    loads[0].wait()
+    vol[...] = vol_raw[...].astype(F32).reshape(64, 512).astype(BF)
+    pl.semaphore_wait(barrier, 23 + 24 + 14)
+
+    push(vol, vin.at[0], 0, block_place(g + 1, sy))
+    push(vol, vin.at[1], 0, block_place(g, sy + 1))
+    push(vol, vin.at[2], 0, block_place(g + 1, sy + 1))
+
     for p in range(4):
         r = lax.broadcasted_iota(jnp.int32, (512, 128), 0)
         perm[:, p * 128 : (p + 1) * 128] = jnp.where(r == 4 * lane_of((512, 128)) + p, 1.0, 0.0).astype(BF)
+    for each in loads[1:]:
+        each.wait()
     for j in range(3):
         w1band[j * 32 : (j + 1) * 32, :] = mm(w1[...], band[j, :108, :]).astype(BF)
     zero = jnp.zeros((96, 128), BF)
@@ -169,41 +191,14 @@
                 g4s[:, at : at + 128] = zero
                 for r in range(4):
                     x3s[r * 96 : (r + 1) * 96, at : at + 128] = zero
-    for t in range(27):
-        wb4_t[t * 32 : (t + 1) * 32, :] = w4[:, (26 - t) * 128 : (27 - t) * 128]
-    wb4_t[864:896, :] = jnp.zeros((32, 128), BF)
-    a2[30] = jnp.zeros((16, 128), BF)
-    a3[1, 13] = jnp.zeros((64, 128), BF)
-    a4[1, 13] = jnp.zeros((32, 128), BF)
-    a2[31] = jnp.zeros((16, 128), BF)
-    for k in range(7):
-        wb4[:, k * 128 : (k + 1) * 128] = wb4_t[k * 128 : (k + 1) * 128, :].astype(F32).T.astype(BF)
     for k in range(14):
         size = 128 if k < 13 else 64
         turned = w3t[k * 128 : k * 128 + size, :]
         w3[:, k * 128 : k * 128 + size] = turned.astype(F32).T.astype(BF)
-    for t in range(27):
-        w3b[:, (26 - t) * 128 : (27 - t) * 128] = w3t[t * 64 : (t + 1) * 64, :]
-    wbk_t[...] = jnp.zeros((512, 256), BF)
-    taps = {(0, 0): 1, (1, 0): 2, (1, 1): 0}
-    for (pa, a), kd in taps.items():
-        for (pb, b), kh in taps.items():
-            for (pe, s), kw in taps.items():
-                r = (a * 4 + b * 2 + s) * 64
-                c = (pa * 4 + pe * 2 + pb) * 32
-                t = (9 * kd + 3 * kh + kw) * 32
-                wbk_t[r : r + 64, c : c + 32] = w2[:, t : t + 32]
-    for r in range(4):
-        for c in range(2):
-            block = wbk_t[r * 128 : (r + 1) * 128, c * 128 : (c + 1) * 128]
-            wbk[c * 128 : (c + 1) * 128, r * 128 : (r + 1) * 128] = block.astype(F32).T.astype(BF)
-
-    pl.semaphore_wait(barrier, 23 + 24 + 14)
-
-    push(vol, vin.at[0], 0, block_place(g + 1, sy))
-    push(vol, vin.at[1], 0, block_place(g, sy + 1))
-    push(vol, vin.at[2], 0, block_place(g + 1, sy + 1))
-
+    for p in range(2):
+        for h in range(4):
+            at = (p * 4 + h) * 128
+            gout[:, at : at + 128] = gout_raw[:, p, h, :]
     await_bytes(vin, recv.at[0])
     none = jnp.zeros((64, 512), BF)
     blocks = jnp.concatenate(
@@ -248,6 +243,31 @@
     push(s2own, s2buf.at[1], 2, block_place(g, sy - 1))
     push(s2own, s2buf.at[2], 2, block_place(g - 1, sy))
     push(s2own, s2buf.at[3], 2, block_place(g - 1, sy - 1))
+    for t in range(27):
+        wb4_t[t * 32 : (t + 1) * 32, :] = w4[:, (26 - t) * 128 : (27 - t) * 128]
+    wb4_t[864:896, :] = jnp.zeros((32, 128), BF)
+    a2[30] = jnp.zeros((16, 128), BF)
+    a3[1, 13] = jnp.zeros((64, 128), BF)
+    a4[1, 13] = jnp.zeros((32, 128), BF)
+    a2[31] = jnp.zeros((16, 128), BF)
+    for k in range(7):
+        wb4[:, k * 128 : (k + 1) * 128] = wb4_t[k * 128 : (k + 1) * 128, :].astype(F32).T.astype(BF)
+    for t in range(27):
+        w3b[:, (26 - t) * 128 : (27 - t) * 128] = w3t[t * 64 : (t + 1) * 64, :]
+    wbk_t[...] = jnp.zeros((512, 256), BF)
+    taps = {(0, 0): 1, (1, 0): 2, (1, 1): 0}
+    for (pa, a), kd in taps.items():
+        for (pb, b), kh in taps.items():
+            for (pe, s), kw in taps.items():
+                r = (a * 4 + b * 2 + s) * 64
+                c = (pa * 4 + pe * 2 + pb) * 32
+                t = (9 * kd + 3 * kh + kw) * 32
+                wbk_t[r : r + 64, c : c + 32] = w2[:, t : t + 32]
+    for r in range(4):
+        for c in range(2):
+            block = wbk_t[r * 128 : (r + 1) * 128, c * 128 : (c + 1) * 128]
+            wbk[c * 128 : (c + 1) * 128, r * 128 : (r + 1) * 128] = block.astype(F32).T.astype(BF)
+
     await_bytes(gath.at[pl.ds(0, 23)], recv.at[1])
 
     def spread_three(ref, rows, at, x, keep):
@@ -286,6 +306,10 @@
         grad = (gout[:, here].astype(F32) * smooth_slope(pre) * scale).astype(BF)
         grads.append(grad)
         g4send[p] = grad
+    stores = [
+        pltpu.make_async_copy(src, dst, load.at[8 + k])
+        for k, (src, dst) in enumerate(((activ, activ_out), (all4, out4), (all3, out3), (all2, out2)))
+    ]
     push(g4send.at[0], g4halo.at[1], 3, (lax.rem(sx + 31, 32), sy, ch))
     push(g4send.at[1], g4halo.at[0], 3, (lax.rem(sx + 1, 32), sy, ch))
     for kd in range(3):
@@ -302,6 +326,7 @@
         for h in range(4):
             x = grads[p][:, h * 128 : (h + 1) * 128].astype(F32)
             spread_three(g4s, 32, ((p + 1) * 6 + h + 1) * 128, x, None)
+    stores[0].start()
     await_bytes(g4halo, recv.at[3])
     for e, p, keep in ((0, 0, sx > 0), (1, 3, sx < 31)):
         for h in range(4):
@@ -451,12 +476,14 @@
     arrived(rank3, all3, 14)
     push(all3.at[core], all3.at[core], 7, mate)
     await_bytes(all4.at[0], recv.at[17])
-    out4[...] = all4[...]
+    stores[1].start()
     await_bytes(all3.at[0], recv.at[7])
-    out3[...] = all3[...]
+    stores[2].start()
     await_bytes(all2.at[pl.ds(0, 31)], recv.at[15])
-    out2[...] = all2[...]
-
+    stores[3].start()
+
+    for each in stores:
+        each.wait()
     await_bytes(vin, send.at[0])
     await_bytes(gath.at[pl.ds(0, 23)], send.at[1])
     await_bytes(s2buf.at[pl.ds(0, 3)], send.at[2])
@@ -523,8 +550,8 @@
             jax.ShapeDtypeStruct((2, HALF, 64, 128), BF),
             jax.ShapeDtypeStruct((2, HALF, 32, 128), BF),
         ),
-        in_specs=[vmem] * 8,
-        out_specs=(vmem,) * 4,
+        in_specs=[pl.BlockSpec(memory_space=pltpu.HBM)] * 8,
+        out_specs=(pl.BlockSpec(memory_space=pltpu.HBM),) * 4,
         scratch_shapes=[
             pltpu.VMEM((512, 512), BF),
             pltpu.VMEM((96, 288), BF),
@@ -570,20 +597,32 @@
             pltpu.VMEM((2, HALF, 64, 128), BF),
             pltpu.VMEM((32, 16, 128), BF),
             pltpu.VMEM((2, HALF, 32, 128), BF),
+            pltpu.VMEM((32, 1024), BF),
+            pltpu.VMEM((4, 4, 4, 512), BF),
+            pltpu.VMEM((32, 2, 4, 128), BF),
+            pltpu.VMEM((64, 512), BF),
+            pltpu.VMEM((32, 108), BF),
+            pltpu.VMEM((64, 864), BF),
+            pltpu.VMEM((1728, 128), BF),
+            pltpu.VMEM((32, 3456), BF),
+            pltpu.VMEM((32, 1024), BF),
+            pltpu.VMEM((224, 256), BF),
+            pltpu.VMEM((3, 128, 288), BF),
             pltpu.SemaphoreType.DMA((18,)),
             pltpu.SemaphoreType.DMA((18,)),
+            pltpu.SemaphoreType.DMA((12,)),
         ],
         compiler_params=pltpu.CompilerParams(
-            collective_id=1, has_side_effects=True, vmem_limit_bytes=48 * 1024 * 1024
+            collective_id=1, has_side_effects=True, vmem_limit_bytes=60 * 1024 * 1024
         ),
         name="forward_and_backward",
     )(
-        volume.reshape(64, 512),
+        volume,
         w_first,
         w_second,
         w_third.T,
         w_deep,
-        grad_out.reshape(32, 1024),
+        grad_out,
         jnp.asarray(row_choice(), BF),
         jnp.asarray(band_choice(), BF),
     )
@@ -596,7 +635,7 @@
             jax.ShapeDtypeStruct((1728, 128), F32),
             jax.ShapeDtypeStruct((32, 3456), F32),
         ),
-        compiler_params=pltpu.CompilerParams(vmem_limit_bytes=32 * 1024 * 1024),
+        compiler_params=pltpu.CompilerParams(vmem_limit_bytes=60 * 1024 * 1024),
         name="widen_outputs",
     )(*outs)
     return (activ, grad_w1, grad_w2, grad_w3.T, grad_w4)

time: 73.3 us -> 69.9 us (0.954)
  local copies, waits for them, and re-layouts: 5.55 us -> 0 us
  Pallas kernels: 66.8 us -> 69.1 us
    unnamed x12 -> x0, local copies, waits for them, and re-layouts: 3.78 us -> none
    reshape x2 -> x0, local copies, waits for them, and re-layouts: 1.78 us -> none  [the longest x1 0.9 us: per_device(): volume.reshape(64, 512)]
    pallas_call x1, Pallas kernels: 1.21 us -> 2.39 us  [per_device(): pl.pallas_call(finish_kernel, out_shape=(jax.ShapeDtypeStruct((32, 2, 4,...]
    pallas_call x1, Pallas kernels: 65.6 us -> 66.8 us  [per_device(): pl.pallas_call(kernel, out_shape=(jax.ShapeDtypeStruct((32, 1024), BF), j...]
where the time goes in v4:
time: 69.9 us; the launch traced here: 69.8 us
  Pallas kernels  69.1 us (99%)
    pallas_call x1, Pallas kernels, per_device(): pl.pallas_call(kernel, out_shape=(jax.ShapeDtypeStruct((32, 1024), BF), j...  66.8 us
    pallas_call x1, Pallas kernels, per_device(): pl.pallas_call(finish_kernel, out_shape=(jax.ShapeDtypeStruct((32, 2, 4,...  2.39 us

profile of v4, /device:TPU:1, one launch (start us, length us, event | category | flops | bytes accessed | tf_op | source)
XLA Modules:
  0.0 69.8 jit_solution(1393941740379988600)
XLA Ops:
  0.6 66.8 %forward_and_backward.1 = (bf16[32,1024]{1,0:T(8,128)(2,1)}, bf16[32,16,128]{2,1,0:T(8,128)(2,1)}, bf16[2,14,64,128]{3,2,1,0:T(8,128)(2,1)}, bf16[2,14,32,128]{3,2,1,0:T(8,128)(2,1)}) custom-call(bf16[4,4,4,512]{3,2,1,0:T(4,128)(2,1)} %refs_0_.1, bf16[32,108]{1,0:T(8,128)(2,1)} %refs_1_.1, bf16[64,864]{1,0:T(8,128)(2,1)} %refs_2_.1, ...), custom_call_target="tpu_custom_call" | custom-call | tf_op jit(solution)/shard_map/forward_and_backward/pallas_call | solution.py:545
  67.4 2.4 %widen_outputs.1 = (bf16[32,2,4,128]{3,2,1,0:T(4,128)(2,1)}, f32[32,108]{1,0:T(8,128)}, f32[64,864]{1,0:T(8,128)}, f32[1728,128]{1,0:T(8,128)}, f32[32,3456]{1,0:T(8,128)}) custom-call(bf16[32,1024]{1,0:T(8,128)(2,1)} %get-tuple-element.14.act, bf16[32,16,128]{2,1,0:T(8,128)(2,1)} %get-tuple-element.15.all2, ...), custom_call_target="tpu_custom_call" | custom-call | tf_op jit(solution)/shard_map/widen_outputs/pallas_call | solution.py:629

commit v5 on v4

--- a/solution.py
+++ b/solution.py
@@ -10,6 +10,7 @@
 BF = jnp.bfloat16
 F32 = jnp.float32
 HALF = 14
+SMALL = 30
 
 
 def row_choice():
@@ -246,10 +247,10 @@
     for t in range(27):
         wb4_t[t * 32 : (t + 1) * 32, :] = w4[:, (26 - t) * 128 : (27 - t) * 128]
     wb4_t[864:896, :] = jnp.zeros((32, 128), BF)
-    a2[30] = jnp.zeros((16, 128), BF)
+    all2[30] = jnp.zeros((16, 128), BF)
     a3[1, 13] = jnp.zeros((64, 128), BF)
     a4[1, 13] = jnp.zeros((32, 128), BF)
-    a2[31] = jnp.zeros((16, 128), BF)
+    all2[31] = jnp.zeros((16, 128), BF)
     for k in range(7):
         wb4[:, k * 128 : (k + 1) * 128] = wb4_t[k * 128 : (k + 1) * 128, :].astype(F32).T.astype(BF)
     for t in range(27):
@@ -360,9 +361,10 @@
     await_bytes(pair4, recv.at[16])
     sum4[...] = (a4[core].astype(F32) + pair4[...].astype(F32)).astype(BF)
     scatter(line, HALF, sum4, in4, rank4, 8)
+    slope_three = smooth_slope(p3[cell])
     rs_recv[cell] = rs_send[cell]
     await_bytes(rs_recv.at[pl.ds(0, 7)], recv.at[4])
-    grad_three = (total(rs_recv) * smooth_slope(p3[cell])).astype(BF)
+    grad_three = (total(rs_recv) * slope_three).astype(BF)
     g3own[...] = grad_three
     g3buf[5] = grad_three
 
@@ -392,6 +394,7 @@
     sum3[...] = (a3[core].astype(F32) + pair3[...].astype(F32)).astype(BF)
     scatter(square, HALF, sum3, in3, rank3, 9)
 
+    p1[...] = smooth_slope(p1[...])
     await_bytes(g3buf.at[pl.ds(0, 15)], recv.at[5])
     for d in range(4):
         for h in range(4):
@@ -413,18 +416,18 @@
             r = (a * 2 + b) * 128
             g2st[r : r + 64, :] = x
             g2st[r + 64 : r + 128, :] = from_right(x.astype(F32)).astype(BF)
-    @pl.when(rank3 < HALF)
-    def _():
-        in3[rank3] = sum3[rank3]
-        await_bytes(in3.at[pl.ds(0, 15)], recv.at[9])
-        part3[...] = total(in3).astype(BF)
-        mid3[z] = part3[...]
-        spread(column, part3, mid3.at[z], 12)
-
+    grad_two = g2st[0:64, :]
+    for k in range(7):
+        size = 128 if k < 6 else 96
+        part = mm_nt(grad_two, a1[k * 128 : k * 128 + size, :]).astype(BF)
+        if k == 6:
+            part = jnp.concatenate([part, jnp.zeros((64, 32), BF)], axis=1)
+        for r in range(4):
+            a2[k * 4 + r] = part[r * 16 : (r + 1) * 16]
+    scatter(plane, 28, a2, in2, rank, 11)
     back_one = mm(wbk[...], g2st[...])
-    slope_one = smooth_slope(p1[...])
     grad_one = jnp.concatenate(
-        [back_one[k * 64 : (k + 1) * 64] * slope_one[:, k * 128 : (k + 1) * 128] for k in range(4)], axis=1
+        [back_one[k * 64 : (k + 1) * 64] * p1[:, k * 128 : (k + 1) * 128] for k in range(4)], axis=1
     ).astype(BF)
     banded = mm_nt(grad_one, vst[:, 256:])
     high = banded.astype(BF)
@@ -436,15 +439,25 @@
     local_one = local_one.astype(BF)
     a2[28] = local_one[:16]
     a2[29] = local_one[16:]
-    grad_two = g2st[0:64, :]
-    for k in range(7):
-        size = 128 if k < 6 else 96
-        part = mm_nt(grad_two, a1[k * 128 : k * 128 + size, :]).astype(BF)
-        if k == 6:
-            part = jnp.concatenate([part, jnp.zeros((64, 32), BF)], axis=1)
-        for r in range(4):
-            a2[k * 4 + r] = part[r * 16 : (r + 1) * 16]
-    scatter(plane, 32, a2, in2, rank, 11)
+    for shard, row in ((28, 0), (29, 1)):
+        @pl.when(rank != shard)
+        def _():
+            push(a2.at[shard], in2.at[rank], 11, (17 + z * 2, row, 1))
+    @pl.when(rank3 < HALF)
+    def _():
+        in3[rank3] = sum3[rank3]
+        await_bytes(in3.at[pl.ds(0, 15)], recv.at[9])
+        part3[...] = total(in3).astype(BF)
+        mid3[z] = part3[...]
+        spread(column, part3, mid3.at[z], 12)
+
+    @pl.when(rank < SMALL)
+    def _():
+        in2[rank] = a2[rank]
+        await_bytes(in2.at[pl.ds(0, 31)], recv.at[11])
+        part2[...] = total(in2).astype(BF)
+        mid2[z] = part2[...]
+        spread(column, part2, mid2.at[z], 13)
 
     @pl.when(rank3 < HALF)
     def _():
@@ -452,15 +465,11 @@
         all3[core, rank3] = total(mid3).astype(BF)
         spread(square, all3.at[core, rank3], all3.at[core, rank3], 14)
 
-    in2[rank] = a2[rank]
-    await_bytes(in2.at[pl.ds(0, 31)], recv.at[11])
-    part2[...] = total(in2).astype(BF)
-    mid2[z] = part2[...]
-    spread(column, part2, mid2.at[z], 13)
-
-    await_bytes(mid2.at[pl.ds(0, 7)], recv.at[13])
-    all2[rank] = total(mid2).astype(BF)
-    spread(plane, all2.at[rank], all2.at[rank], 15)
+    @pl.when(rank < SMALL)
+    def _():
+        await_bytes(mid2.at[pl.ds(0, 7)], recv.at[13])
+        all2[rank] = total(mid2).astype(BF)
+        spread(plane, all2.at[rank], all2.at[rank], 15)
 
     def arrived(me, buf, slot):
         @pl.when(me < HALF)
@@ -479,7 +488,14 @@
     stores[1].start()
     await_bytes(all3.at[0], recv.at[7])
     stores[2].start()
-    await_bytes(all2.at[pl.ds(0, 31)], recv.at[15])
+    @pl.when(rank < SMALL)
+    def _():
+        await_bytes(all2.at[pl.ds(0, SMALL - 1)], recv.at[15])
+
+    @pl.when(rank >= SMALL)
+    def _():
+        await_bytes(all2.at[pl.ds(0, SMALL)], recv.at[15])
+
     stores[3].start()
 
     for each in stores:
@@ -491,7 +507,16 @@
     await_bytes(rs_send.at[pl.ds(0, 7)], send.at[4])
     await_bytes(g3buf.at[pl.ds(0, 15)], send.at[5])
 
-    await_bytes(in2.at[pl.ds(0, 31)], send.at[11])
+    @pl.when(rank < SMALL)
+    def _():
+        await_bytes(a2.at[pl.ds(0, SMALL - 1)], send.at[11])
+        await_bytes(mid2.at[pl.ds(0, 7)], send.at[13])
+        await_bytes(in2.at[pl.ds(0, 31)], send.at[15])
+
+    @pl.when(rank >= SMALL)
+    def _():
+        await_bytes(a2.at[pl.ds(0, SMALL)], send.at[11])
+
     for pair, total_sum, gathered, slots in ((pair4, sum4, all4, (16, 8, 10, 17)), (pair3, sum3, all3, (6, 9, 14, 7))):
         me = rank4 if pair is pair4 else rank3
         await_bytes(pair, send.at[slots[0]])
@@ -514,24 +539,48 @@
         await_bytes(mid3.at[pl.ds(0, 7)], send.at[12])
         await_bytes(in3.at[pl.ds(0, 15)], send.at[14])
 
-    await_bytes(mid2.at[pl.ds(0, 7)], send.at[13])
-    await_bytes(in2.at[pl.ds(0, 31)], send.at[15])
-
-
-def finish_kernel(act, all2, all3, all4, activ, o1, o2, o3, o4):
+
+def finish_kernel(
+    act_in, in2, in3, in4, activ_out, out1, out2, out3, out4,
+    act, all2, all3, all4, activ, o1, o2, o3, o4, come, leave,
+):
+    loads = [
+        pltpu.make_async_copy(src, dst, come.at[k])
+        for k, (src, dst) in enumerate(((in4, all4), (in3, all3), (act_in, act), (in2, all2)))
+    ]
+    stores = [
+        pltpu.make_async_copy(src, dst, leave.at[k])
+        for k, (src, dst) in enumerate(
+            ((o4, out4), (o3, out3), (activ, activ_out), (o2, out2), (o1, out1))
+        )
+    ]
+    for each in loads:
+        each.start()
+    loads[0].wait()
+    for t in range(27):
+        o4[:, t * 128 : (t + 1) * 128] = all4[t // HALF, t % HALF].astype(F32)
+    stores[0].start()
+    loads[1].wait()
+    for t in range(27):
+        o3[t * 64 : (t + 1) * 64, :] = all3[t // HALF, t % HALF].astype(F32)
+    stores[1].start()
+    loads[2].wait()
     for p in range(2):
         for h in range(4):
             at = (p * 4 + h) * 128
             activ[:, p, h, :] = act[:, at : at + 128]
-    for t in range(27):
-        o4[:, t * 128 : (t + 1) * 128] = all4[t // HALF, t % HALF].astype(F32)
-        o3[t * 64 : (t + 1) * 64, :] = all3[t // HALF, t % HALF].astype(F32)
+    stores[2].start()
+    loads[3].wait()
     for k in range(7):
         size = 128 if k < 6 else 96
         for r in range(4):
             o2[r * 16 : (r + 1) * 16, k * 128 : k * 128 + size] = all2[k * 4 + r].astype(F32)[:, :size]
+    stores[3].start()
     o1[0:16, :] = all2[28].astype(F32)[:, :108]
     o1[16:32, :] = all2[29].astype(F32)[:, :108]
+    stores[4].start()
+    for each in stores:
+        each.wait()
 
 
 def per_device(volume, w_first, w_second, w_third, w_deep, grad_out):
@@ -635,6 +684,21 @@
             jax.ShapeDtypeStruct((1728, 128), F32),
             jax.ShapeDtypeStruct((32, 3456), F32),
         ),
+        in_specs=[pl.BlockSpec(memory_space=pltpu.HBM)] * 4,
+        out_specs=(pl.BlockSpec(memory_space=pltpu.HBM),) * 5,
+        scratch_shapes=[
+            pltpu.VMEM((32, 1024), BF),
+            pltpu.VMEM((32, 16, 128), BF),
+            pltpu.VMEM((2, HALF, 64, 128), BF),
+            pltpu.VMEM((2, HALF, 32, 128), BF),
+            pltpu.VMEM((32, 2, 4, 128), BF),
+            pltpu.VMEM((32, 108), F32),
+            pltpu.VMEM((64, 864), F32),
+            pltpu.VMEM((1728, 128), F32),
+            pltpu.VMEM((32, 3456), F32),
+            pltpu.SemaphoreType.DMA((4,)),
+            pltpu.SemaphoreType.DMA((5,)),
+        ],
         compiler_params=pltpu.CompilerParams(vmem_limit_bytes=60 * 1024 * 1024),
         name="widen_outputs",
     )(*outs)

time: 69.9 us -> 68.9 us (0.986)
  Pallas kernels: 69.1 us -> 68.2 us
    pallas_call x1, Pallas kernels: 66.8 us -> 65.9 us  [per_device(): pl.pallas_call(kernel, out_shape=(jax.ShapeDtypeStruct((32, 1024), BF), j...]
where the time goes in v5:
time: 68.9 us; the launch traced here: 68.8 us
  Pallas kernels  68.2 us (99%)
    pallas_call x1, Pallas kernels, per_device(): pl.pallas_call(kernel, out_shape=(jax.ShapeDtypeStruct((32, 1024), BF), j...  65.9 us
    pallas_call x1, Pallas kernels, per_device(): pl.pallas_call(finish_kernel, out_shape=(jax.ShapeDtypeStruct((32, 2, 4,...  2.28 us

profile of v5, /device:TPU:1, one launch (start us, length us, event | category | flops | bytes accessed | tf_op | source)
XLA Modules:
  0.0 68.8 jit_solution(591168405584300064)
XLA Ops:
  0.6 65.9 %forward_and_backward.1 = (bf16[32,1024]{1,0:T(8,128)(2,1)}, bf16[32,16,128]{2,1,0:T(8,128)(2,1)}, bf16[2,14,64,128]{3,2,1,0:T(8,128)(2,1)}, bf16[2,14,32,128]{3,2,1,0:T(8,128)(2,1)}) custom-call(bf16[4,4,4,512]{3,2,1,0:T(4,128)(2,1)} %refs_0_.1, bf16[32,108]{1,0:T(8,128)(2,1)} %refs_1_.1, bf16[64,864]{1,0:T(8,128)(2,1)} %refs_2_.1, ...), custom_call_target="tpu_custom_call" | custom-call | tf_op jit(solution)/shard_map/forward_and_backward/pallas_call | solution.py:594
  66.5 2.3 %widen_outputs.1 = (bf16[32,2,4,128]{3,2,1,0:T(4,128)(2,1)}, f32[32,108]{1,0:T(8,128)}, f32[64,864]{1,0:T(8,128)}, f32[1728,128]{1,0:T(8,128)}, f32[32,3456]{1,0:T(8,128)}) custom-call(bf16[32,1024]{1,0:T(8,128)(2,1)} %get-tuple-element.14.act_in, bf16[32,16,128]{2,1,0:T(8,128)(2,1)} %get-tuple-element.15.in2, ...), custom_call_target="tpu_custom_call" | custom-call | tf_op jit(solution)/shard_map/widen_outputs/pallas_call | solution.py:678

commit v6 on v5

--- a/solution.py
+++ b/solution.py
@@ -396,19 +396,23 @@
 
     p1[...] = smooth_slope(p1[...])
     await_bytes(g3buf.at[pl.ds(0, 15)], recv.at[5])
-    for d in range(4):
-        for h in range(4):
-            keep = (g - 1 + d >= 0) & (g - 1 + d < 64) & (sy - 1 + h >= 0) & (sy - 1 + h < 4)
-            spread_three(g3s, 128, (d * 4 + h) * 128, g3buf[d * 4 + h].astype(F32), keep)
-    await_bytes(s2buf.at[pl.ds(0, 3)], recv.at[2])
-    for a in range(2):
+
+    def spread_grad(d, h):
+        keep = (g - 1 + d >= 0) & (g - 1 + d < 64) & (sy - 1 + h >= 0) & (sy - 1 + h < 4)
+        spread_three(g3s, 128, (d * 4 + h) * 128, g3buf[d * 4 + h].astype(F32), keep)
+
+    def back_two(a, first, count):
         around = jnp.concatenate(
-            [g3s[:, ((a + kd) * 4 + kh) * 128 : ((a + kd) * 4 + kh + 2) * 128] for kd in range(3) for kh in range(3)],
+            [
+                g3s[:, ((a + kd) * 4 + kh + first) * 128 : ((a + kd) * 4 + kh + first + count) * 128]
+                for kd in range(3)
+                for kh in range(3)
+            ],
             axis=0,
         )
         back = mm(w3b[...], around)
-        for b in range(2):
-            x = back[:, b * 128 : (b + 1) * 128] * s2buf[a * 2 + b]
+        for b in range(first, first + count):
+            x = back[:, (b - first) * 128 : (b - first + 1) * 128] * s2buf[a * 2 + b]
             if a or b:
                 keep = (g + a < 64) & (sy + b < 4)
                 x = jnp.where(keep, x, 0.0)
@@ -416,6 +420,12 @@
             r = (a * 2 + b) * 128
             g2st[r : r + 64, :] = x
             g2st[r + 64 : r + 128, :] = from_right(x.astype(F32)).astype(BF)
+
+    for d in range(3):
+        for h in range(3):
+            spread_grad(d, h)
+    await_bytes(s2buf.at[pl.ds(0, 3)], recv.at[2])
+    back_two(0, 0, 1)
     grad_two = g2st[0:64, :]
     for k in range(7):
         size = 128 if k < 6 else 96
@@ -425,6 +435,12 @@
         for r in range(4):
             a2[k * 4 + r] = part[r * 16 : (r + 1) * 16]
     scatter(plane, 28, a2, in2, rank, 11)
+    for k in range(3):
+        spread_grad(k, 3)
+    for h in range(4):
+        spread_grad(3, h)
+    back_two(0, 1, 1)
+    back_two(1, 0, 2)
     back_one = mm(wbk[...], g2st[...])
     grad_one = jnp.concatenate(
         [back_one[k * 64 : (k + 1) * 64] * p1[:, k * 128 : (k + 1) * 128] for k in range(4)], axis=1

time: 68.9 us -> 68.5 us (level)
  no operation moved by 1% of the time
where the time goes in v6:
time: 68.5 us; the launch traced here: 68.4 us
  Pallas kernels  67.8 us (99%)
    pallas_call x1, Pallas kernels, per_device(): pl.pallas_call(kernel, out_shape=(jax.ShapeDtypeStruct((32, 1024), BF), j...  65.5 us
    pallas_call x1, Pallas kernels, per_device(): pl.pallas_call(finish_kernel, out_shape=(jax.ShapeDtypeStruct((32, 2, 4,...  2.28 us

profile of v6, /device:TPU:1, one launch (start us, length us, event | category | flops | bytes accessed | tf_op | source)
XLA Modules:
  0.0 68.4 jit_solution(1209166431734030642)
XLA Ops:
  0.6 65.5 %forward_and_backward.1 = (bf16[32,1024]{1,0:T(8,128)(2,1)}, bf16[32,16,128]{2,1,0:T(8,128)(2,1)}, bf16[2,14,64,128]{3,2,1,0:T(8,128)(2,1)}, bf16[2,14,32,128]{3,2,1,0:T(8,128)(2,1)}) custom-call(bf16[4,4,4,512]{3,2,1,0:T(4,128)(2,1)} %refs_0_.1, bf16[32,108]{1,0:T(8,128)(2,1)} %refs_1_.1, bf16[64,864]{1,0:T(8,128)(2,1)} %refs_2_.1, ...), custom_call_target="tpu_custom_call" | custom-call | tf_op jit(solution)/shard_map/forward_and_backward/pallas_call | solution.py:610
  66.1 2.3 %widen_outputs.1 = (bf16[32,2,4,128]{3,2,1,0:T(4,128)(2,1)}, f32[32,108]{1,0:T(8,128)}, f32[64,864]{1,0:T(8,128)}, f32[1728,128]{1,0:T(8,128)}, f32[32,3456]{1,0:T(8,128)}) custom-call(bf16[32,1024]{1,0:T(8,128)(2,1)} %get-tuple-element.14.act_in, bf16[32,16,128]{2,1,0:T(8,128)(2,1)} %get-tuple-element.15.in2, ...), custom_call_target="tpu_custom_call" | custom-call | tf_op jit(solution)/shard_map/widen_outputs/pallas_call | solution.py:694
